TPU v7x, 32 devices: a whole 2x2x4 slice. The times are simulated.
32 devices in a mesh: dp: 16 (over z, y, x), tensor: 2 (over core).
Axes of the slice: x: 2, y: 2, z: 4, core: 2. Of those that a mesh axis runs over, the one named last changes fastest.
Arguments:
- tokens: bfloat16 [32768, 1024], P(('dp', 'tensor')), may hold values from -6 to 6
- norm_gain1: float32 [1024], replicated, may hold values from 0.1 to 1.9
- in_weight: bfloat16 [1024, 3, 1024], P('dp', None, 'tensor'), may hold values from -0.1875 to 0.1875
- conv_kernel: bfloat16 [3, 1024], P(None, 'tensor'), may hold values from -3.5 to 3.5
- out_weight: bfloat16 [1024, 1024], P('dp', 'tensor'), may hold values from -0.1875 to 0.1875
- norm_gain2: float32 [1024], replicated, may hold values from 0.1 to 1.9
- gate_up_weight: bfloat16 [1024, 2, 4608], P('dp', None, 'tensor'), may hold values from -0.1875 to 0.1875
- down_weight: bfloat16 [1024, 4608], P('dp', 'tensor'), may hold values from -0.09375 to 0.09375
- out_grad: bfloat16 [32768, 1024], P(('dp', 'tensor')), may hold values from -6 to 6
Outputs:
- mixed_out: bfloat16 [32768, 1024], P(('dp', 'tensor'))
- input_grad: float32 [32768, 1024], P(('dp', 'tensor'))
- gain1_grad: float32 [1024], replicated
- in_weight_grad: float32 [1024, 3, 1024], P('dp', None, 'tensor')
- conv_grad: float32 [3, 1024], P(None, 'tensor')
- out_weight_grad: float32 [1024, 1024], P('dp', 'tensor')
- gain2_grad: float32 [1024], replicated
- gate_up_grad: float32 [1024, 2, 4608], P('dp', None, 'tensor')
- down_grad: float32 [1024, 4608], P('dp', 'tensor')
All inputs are finite; a program needn't handle non-finite values.
Results may differ from a plain program's by a relative error of at most 0.011.
Values may be sent and summed in bfloat16 or wider, within the bound.
No kernel may reach another device: no remote copies, remote signals or barrier semaphores. Data moves between devices by JAX's collectives and lax.ppermute only.
A program may use at most 320 MiB of HBM per device.

v0:
```python
import jax
import jax.numpy as jnp
from jax import lax
from jax.sharding import PartitionSpec as P

LEN = 1024


eps = 1e-05


def rms_forward(stream, norm_gain):
    inverse = lax.rsqrt(jnp.mean(stream * stream, axis=-1, keepdims=True) + eps)
    unit_rows = stream * inverse
    return (unit_rows * norm_gain, unit_rows, inverse)


def rms_backward(grad_normed, unit_rows, inverse, norm_gain):
    gain_grad = jnp.sum(grad_normed * unit_rows, axis=0)
    grad_unit = grad_normed * norm_gain
    along = jnp.mean(grad_unit * unit_rows, axis=-1, keepdims=True)
    return (inverse * (grad_unit - unit_rows * along), gain_grad)


def causal_conv(values, kernel):
    channels = values.shape[-1]
    blocks = values.reshape(-1, LEN, channels)
    padded = jnp.pad(blocks, ((0, 0), (2, 0), (0, 0)))
    summed = (
        kernel[0] * padded[:, 0:LEN]
        + kernel[1] * padded[:, 1 : LEN + 1]
        + kernel[2] * padded[:, 2 : LEN + 2]
    )
    return summed.reshape(values.shape)


def conv_backward(grad_out, values, kernel):
    channels = values.shape[-1]
    grad_blocks = grad_out.reshape(-1, LEN, channels)
    padded = jnp.pad(values.reshape(-1, LEN, channels), ((0, 0), (2, 0), (0, 0)))
    kernel_grad = jnp.stack(
        [
            jnp.sum(grad_blocks * padded[:, 0:LEN], axis=(0, 1)),
            jnp.sum(grad_blocks * padded[:, 1 : LEN + 1], axis=(0, 1)),
            jnp.sum(grad_blocks * padded[:, 2 : LEN + 2], axis=(0, 1)),
        ]
    )
    later = jnp.pad(grad_blocks, ((0, 0), (0, 2), (0, 0)))
    grad_values = (
        kernel[0] * later[:, 2 : LEN + 2]
        + kernel[1] * later[:, 1 : LEN + 1]
        + kernel[2] * later[:, 0:LEN]
    )
    return (grad_values.reshape(values.shape), kernel_grad)


def mixer_forward(normed_rows, in_w, kernel):
    projected = jnp.einsum("td,dkc->tkc", normed_rows, in_w, preferred_element_type=jnp.float32)
    mixed_in = projected[:, 0] * projected[:, 2]
    convolved = causal_conv(mixed_in, kernel)
    gated = (projected[:, 1] * convolved).astype(jnp.bfloat16)
    return (projected, mixed_in, convolved, gated)


def mixer_backward(grad_gated, projected, mixed_in, convolved, kernel):
    grad_c = grad_gated * convolved
    grad_conv = grad_gated * projected[:, 1]
    grad_mixed, kernel_grad = conv_backward(grad_conv, mixed_in, kernel)
    grad_stack = jnp.stack(
        [grad_mixed * projected[:, 2], grad_c, grad_mixed * projected[:, 0]], axis=1
    )
    return (grad_stack.astype(jnp.bfloat16), kernel_grad)


def ffn_forward(normed_rows, gate_up_w):
    gate_up = jnp.einsum("td,dkf->tkf", normed_rows, gate_up_w, preferred_element_type=jnp.float32)
    hidden = (jax.nn.silu(gate_up[:, 0]) * gate_up[:, 1]).astype(jnp.bfloat16)
    return (gate_up, hidden)


def ffn_backward(grad_hidden, gate_up):
    gate = gate_up[:, 0]
    sigm = jax.nn.sigmoid(gate)
    grad_up = grad_hidden * gate * sigm
    grad_gate = grad_hidden * gate_up[:, 1] * sigm * (1.0 + gate * (1.0 - sigm))
    return jnp.stack([grad_gate, grad_up], axis=1).astype(jnp.bfloat16)


def run_layer(
    tokens,
    out_grad,
    gain_one,
    gain_two,
    in_w,
    kernel_b,
    out_w,
    gate_up_w,
    down_w,
    mixer_movers,
    ffn_movers,
):
    collect_first, reduce_first, collect_grad1, reduce_back1 = mixer_movers
    collect_second, reduce_second, reduce_back2 = ffn_movers
    own_rows = tokens.shape[0]
    kernel = kernel_b.astype(jnp.float32)
    stream = tokens.astype(jnp.float32)
    normed1, unit1, inverse1 = rms_forward(stream, gain_one)
    group_n1 = collect_first(normed1.astype(jnp.bfloat16))
    projected, mixed_in, convolved, gated = mixer_forward(group_n1, in_w, kernel)

    def mix_term(first_row, row_count):
        return jnp.einsum("tc,jc->tj", gated, out_w, preferred_element_type=jnp.float32)

    middle = stream + reduce_first(mix_term, own_rows)
    normed2, unit2, inverse2 = rms_forward(middle, gain_two)
    group_n2, group_grad = collect_second((normed2.astype(jnp.bfloat16), out_grad))
    gate_up, hidden = ffn_forward(group_n2, gate_up_w)

    def ffn_term(first_row, row_count):
        return jnp.einsum("tf,jf->tj", hidden, down_w, preferred_element_type=jnp.float32)

    result = (middle + reduce_second(ffn_term, own_rows)).astype(jnp.bfloat16)
    grad_hidden = jnp.dot(group_grad, down_w, preferred_element_type=jnp.float32)
    down_grad_w = jnp.einsum("tj,tf->jf", group_grad, hidden, preferred_element_type=jnp.float32)
    grad_gate_up = ffn_backward(grad_hidden, gate_up)
    gate_up_grad_w = jnp.einsum(
        "td,tkf->dkf", group_n2, grad_gate_up, preferred_element_type=jnp.float32
    )

    def ffn_back_term(first_row, row_count):
        return jnp.einsum(
            "tkf,dkf->td", grad_gate_up, gate_up_w, preferred_element_type=jnp.float32
        )

    grad_normed2 = reduce_back2(ffn_back_term, own_rows)
    grad_rms2, gain_two_grad = rms_backward(grad_normed2, unit2, inverse2, gain_two)
    grad_middle = out_grad.astype(jnp.float32) + grad_rms2
    group_gm = collect_grad1(grad_middle.astype(jnp.bfloat16))
    out_grad_w = jnp.einsum("tj,tc->jc", group_gm, gated, preferred_element_type=jnp.float32)
    grad_gated = jnp.einsum("tj,jc->tc", group_gm, out_w, preferred_element_type=jnp.float32)
    grad_projected, kernel_grad = mixer_backward(grad_gated, projected, mixed_in, convolved, kernel)
    in_grad_w = jnp.einsum(
        "td,tkc->dkc", group_n1, grad_projected, preferred_element_type=jnp.float32
    )

    def mixer_back_term(first_row, row_count):
        return jnp.einsum("tkc,dkc->td", grad_projected, in_w, preferred_element_type=jnp.float32)

    grad_normed1 = reduce_back1(mixer_back_term, own_rows)
    grad_rms1, gain_one_grad = rms_backward(grad_normed1, unit1, inverse1, gain_one)
    input_grad = grad_middle + grad_rms1
    return (
        result,
        input_grad,
        (gain_one_grad, gain_two_grad),
        (in_grad_w, out_grad_w),
        (gate_up_grad_w, down_grad_w),
        kernel_grad,
    )


def per_device(
    tokens,
    norm_gain1,
    in_weight,
    conv_kernel,
    out_weight,
    norm_gain2,
    gate_up_weight,
    down_weight,
    out_grad,
):
    channels = in_weight.shape[2]
    model_width = tokens.shape[1]
    in_part, out_part, gate_up_part, down_part = (
        lax.all_gather(in_weight, "dp", axis=0, tiled=True),
        lax.all_gather(out_weight, "dp", axis=0, tiled=True),
        lax.all_gather(gate_up_weight, "dp", axis=0, tiled=True),
        lax.all_gather(down_weight, "dp", axis=0, tiled=True),
    )
    in_use, out_use, kernel_use = (in_part, out_part, conv_kernel)

    def collect_first(values):
        return lax.all_gather(values, "tensor", axis=0, tiled=True)

    def reduce_first(term_fn, row_count):
        return lax.psum_scatter(
            term_fn(jnp.int32(0), lax.axis_size("tensor") * row_count),
            "tensor",
            scatter_dimension=0,
            tiled=True,
        )

    def collect_grad1(values):
        return lax.all_gather(values, "tensor", axis=0, tiled=True)

    def reduce_back1(term_fn, row_count):
        return lax.psum_scatter(
            term_fn(jnp.int32(0), lax.axis_size("tensor") * row_count),
            "tensor",
            scatter_dimension=0,
            tiled=True,
        )

    mixer_movers = (collect_first, reduce_first, collect_grad1, reduce_back1)
    gate_up_use, down_use = (gate_up_part, down_part)

    def collect_second(values):
        return (
            lax.all_gather(values[0], "tensor", axis=0, tiled=True),
            lax.all_gather(values[1], "tensor", axis=0, tiled=True),
        )

    def reduce_second(term_fn, row_count):
        return lax.psum_scatter(
            term_fn(jnp.int32(0), lax.axis_size("tensor") * row_count),
            "tensor",
            scatter_dimension=0,
            tiled=True,
        )

    def reduce_back2(term_fn, row_count):
        return lax.psum_scatter(
            term_fn(jnp.int32(0), lax.axis_size("tensor") * row_count),
            "tensor",
            scatter_dimension=0,
            tiled=True,
        )

    ffn_movers = (collect_second, reduce_second, reduce_back2)
    result, input_grad, gain_grads, mixer_grads, ffn_grads, kernel_grad = run_layer(
        tokens,
        out_grad,
        norm_gain1,
        norm_gain2,
        in_use,
        kernel_use,
        out_use,
        gate_up_use,
        down_use,
        mixer_movers,
        ffn_movers,
    )
    in_share, out_share = mixer_grads
    offset = lax.axis_index("tensor") * channels
    kernel_full = lax.dynamic_update_slice(
        jnp.zeros((3, model_width), jnp.float32), kernel_grad, (jnp.int32(0), offset)
    )
    gate_up_share, down_share = ffn_grads
    in_final, out_final, gate_up_final, down_final = (
        lax.psum_scatter(in_share, "dp", scatter_dimension=0, tiled=True),
        lax.psum_scatter(out_share, "dp", scatter_dimension=0, tiled=True),
        lax.psum_scatter(gate_up_share, "dp", scatter_dimension=0, tiled=True),
        lax.psum_scatter(down_share, "dp", scatter_dimension=0, tiled=True),
    )
    gain_one_sum, gain_two_sum, kernel_sum = lax.psum(
        (gain_grads[0], gain_grads[1], kernel_full), ("dp", "tensor")
    )
    conv_share = lax.dynamic_slice_in_dim(
        kernel_sum, lax.axis_index("tensor") * channels, channels, 1
    )
    return (
        result,
        input_grad,
        gain_one_sum,
        in_final,
        conv_share,
        out_final,
        gain_two_sum,
        gate_up_final,
        down_final,
    )


def solution(mesh):
    return jax.shard_map(
        per_device,
        mesh=mesh,
        in_specs=(
            P(("dp", "tensor"), None),
            P(),
            P("dp", None, "tensor"),
            P(None, "tensor"),
            P("dp", "tensor"),
            P(),
            P("dp", None, "tensor"),
            P("dp", "tensor"),
            P(("dp", "tensor"), None),
        ),
        out_specs=(
            P(("dp", "tensor"), None),
            P(("dp", "tensor"), None),
            P(),
            P("dp", None, "tensor"),
            P(None, "tensor"),
            P("dp", "tensor"),
            P(),
            P("dp", None, "tensor"),
            P("dp", "tensor"),
        ),
        check_vma=False,
    )
```

profile of v0, /device:TPU:0, one launch (start us, length us, event | category | flops | bytes accessed | tf_op | source)
XLA Modules:
  0.0 1310.2 jit_solution(9053516311373944407)
XLA Ops:
  15.0 14.9 %all-gather.9.cloned.1.call-done = bf16[2048,1024]{1,0:T(8,128)(2,1)} async-done(((bf16[1024,1024]{1,0:T(8,128)(2,1)}), bf16[2048,1024]{1,0:T(8,128)(2,1)}) %all-gather.9.cloned.1.call-update) | async-done | bytes 4194320 | tf_op jit(solution)/shard_map/all_gather | solution.py:184
  29.9 71.6 %all-gather.11.cloned.1.call-done = bf16[1024,3,512]{2,0,1:T(8,128)(2,1)} async-done(((bf16[64,3,512]{2,0,1:T(8,128)(2,1)}), bf16[1024,3,512]{2,0,1:T(8,128)(2,1)}) %all-gather.11.cloned.1.call-update) | async-done | bytes 3145744 | tf_op jit(solution)/shard_map/all_gather | solution.py:176
  101.5 9.4 fusion.26
  121.5 37.2 %all-gather.13.cloned.1.call-done = bf16[1024,512]{1,0:T(8,128)(2,1)} async-done(((bf16[64,512]{1,0:T(8,128)(2,1)}), bf16[1024,512]{1,0:T(8,128)(2,1)}) %all-gather.13.cloned.1.call-update) | async-done | bytes 1048592 | tf_op jit(solution)/shard_map/all_gather | solution.py:177
  158.6 7.5 fusion.36
  168.2 13.8 %reduce-scatter.11.cloned.1.call-done = f32[1024,1024]{1,0:T(8,128)} async-done(((f32[2048,1024]{1,0:T(8,128)}), f32[1024,1024]{1,0:T(8,128)}) %reduce-scatter.11.cloned.1.call-update) | async-done | bytes 4194320 | tf_op jit(solution)/shard_map/reduce_scatter | solution.py:187
  190.4 118.7 %all-gather.17.cloned.1.call-done = bf16[1024,2,2304]{2,0,1:T(8,128)(2,1)} async-done(((bf16[64,2,2304]{2,0,1:T(8,128)(2,1)}), bf16[1024,2,2304]{2,0,1:T(8,128)(2,1)}) %all-gather.17.cloned.1.call-update) | async-done | bytes 9437200 | tf_op jit(solution)/shard_map/all_gather | solution.py:178
  309.1 13.4 %all-gather.15.cloned.1.call-done = bf16[2048,1024]{1,0:T(8,128)(2,1)} async-done(((bf16[1024,1024]{1,0:T(8,128)(2,1)}), bf16[2048,1024]{1,0:T(8,128)(2,1)}) %all-gather.15.cloned.1.call-update) | async-done | bytes 4194320 | tf_op jit(solution)/shard_map/all_gather | solution.py:210
  322.5 28.1 %fusion.20 = f32[2048,2,2304]{2,0,1:T(8,128)} fusion(bf16[1024,2,2304]{2,0,1:T(8,128)(2,1)} %all-gather.17.cloned.1.call-done, bf16[2048,1024]{1,0:T(8,128)(2,1)} %all-gather.15.cloned.1.call-done), kind=kOutput, calls=%fused_computation.37 | convolution fusion | flops 19327352832 | bytes 51380224 | tf_op jit(solution)/shard_map/td,dkf->tkf/dot_general | solution.py:76
  350.5 73.3 %all-gather.19.cloned.1.call-done = bf16[1024,2304]{1,0:T(8,128)(2,1)} async-done(((bf16[64,2304]{1,0:T(8,128)(2,1)}), bf16[1024,2304]{1,0:T(8,128)(2,1)}) %all-gather.19.cloned.1.call-update) | async-done | bytes 4718608 | tf_op jit(solution)/shard_map/all_gather | solution.py:179
  423.8 35.4 %fusion.3 = (bf16[2048,1,2304]{2,0,1:T(8,128)(2,1)}, bf16[2048,1,2304]{2,0,1:T(8,128)(2,1)}, bf16[2048,2304]{1,0:T(8,128)(2,1)}) fusion(f32[2048,2,2304]{2,0,1:T(8,128)} %fusion.20, bf16[2048,1024]{1,0:T(8,128)(2,1)} %all-gather.21.cloned.1.call-done, bf16[1024,2304]{1,0:T(8,128)(2,1)} %all-gather.19.cloned.1.call-done), kind=kOutput, calls=%fused_computation.10 | convolution fusion | flops 9739173888 | bytes 74973184 | tf_op jit(solution)/shard_map/dot_general | solution.py:123
  459.2 37.6 %fusion.8 = f32[2048,1024]{1,0:T(8,128)} fusion(bf16[1024,2,2304]{2,0,1:T(8,128)(2,1)} %all-gather.17.cloned.1.call-done, bf16[2048,1,2304]{2,0,1:T(8,128)(2,1)} %get-tuple-element.40, bf16[2048,1,2304]{2,0,1:T(8,128)(2,1)} %get-tuple-element.39), kind=kOutput, calls=%fused_computation.20 | convolution fusion | flops 19336790016 | bytes 36700160 | tf_op jit(solution)/shard_map/tkf,dkf->td/dot_general | solution.py:131
  496.9 15.5 %reduce-scatter.15.cloned.1.call-done = f32[1024,1024]{1,0:T(8,128)} async-done(((f32[2048,1024]{1,0:T(8,128)}), f32[1024,1024]{1,0:T(8,128)}) %reduce-scatter.15.cloned.1.call-update) | async-done | bytes 4194320 | tf_op jit(solution)/shard_map/reduce_scatter | solution.py:223
  512.4 4.7 multiply_reduce_fusion
  520.9 15.0 %all-gather.23.cloned.1.call-done = bf16[2048,1024]{1,0:T(8,128)(2,1)} async-done(((bf16[1024,1024]{1,0:T(8,128)(2,1)}), bf16[2048,1024]{1,0:T(8,128)(2,1)}) %all-gather.23.cloned.1.call-update) | async-done | bytes 4194320 | tf_op jit(solution)/shard_map/all_gather | solution.py:195
  536.0 9.7 multiply_reduce_fusion.2
  545.7 7.5 fusion.16
  553.2 6.6 multiply_add_fusion
  559.8 5.7 fusion.17
  567.6 8.8 convolution_bitcast_fusion.1
  576.5 16.4 %fusion.37 = f32[2048,1024]{1,0:T(8,128)} fusion(bf16[2048,2304]{1,0:T(8,128)(2,1)} %get-tuple-element.41, bf16[1024,2304]{1,0:T(8,128)(2,1)} %all-gather.19.cloned.1.call-done), kind=kOutput, calls=%fused_computation.74 | convolution fusion | flops 9663676416 | bytes 22544384 | tf_op jit(solution)/shard_map/tf,jf->tj/dot_general | solution.py:120
  592.9 27.3 %fusion = f32[1024,2,2304]{2,0,1:T(8,128)} fusion(bf16[2048,1,2304]{2,0,1:T(8,128)(2,1)} %get-tuple-element.40, bf16[2048,1,2304]{2,0,1:T(8,128)(2,1)} %get-tuple-element.39, bf16[2048,1024]{1,0:T(8,128)(2,1)} %all-gather.15.cloned.1.call-done), kind=kOutput, calls=%fused_computation.7 | convolution fusion | flops 19365101568 | bytes 41943040 | tf_op jit(solution)/shard_map/td,tkf->dkf/dot_general | solution.py:126
  620.3 16.5 %convolution_bitcast_fusion = f32[1024,2304]{0,1:T(8,128)} fusion(bf16[2048,2304]{1,0:T(8,128)(2,1)} %get-tuple-element.41, bf16[2048,1024]{1,0:T(8,128)(2,1)} %all-gather.21.cloned.1.call-done), kind=kOutput, calls=%fused_computation.11 | convolution fusion | flops 9663676416 | bytes 23068672 | tf_op jit(solution)/shard_map/tj,tf->jf/dot_general | solution.py:124
  636.7 9.7 copy.32
  646.5 6.6 fusion.38
  653.2 11.9 fusion.24
  670.1 44.9 %all-reduce.2 = (f32[1024]{0:T(1024)}, f32[3,1024]{1,0:T(4,128)S(1)}, f32[1024]{0:T(1024)}) all-reduce(f32[1024]{0:T(1024)S(1)} %get-tuple-element.31, f32[3,1024]{1,0:T(4,128)S(1)} %maximum_dynamic-update-slice_fusion, f32[1024]{0:T(1024)S(1)} %get-tuple-element.27), channel_id=1, replica_groups=mesh['dp'=16,'tensor'=2] {'dp','tensor'}, use_global_device_ids=true, to_apply=%region_9.10 | all-reduce | flops 5120 | bytes 40960 | tf_op jit(solution)/shard_map/psum | solution.py:256
  715.6 10.6 fusion.13
  726.2 182.4 %reduce-scatter.23.cloned.1.call-done = f32[64,2,2304]{2,0,1:T(8,128)} async-done(((f32[1024,2,2304]{2,0,1:T(8,128)}), f32[64,2,2304]{2,0,1:T(8,128)}) %reduce-scatter.23.cloned.1.call-update) | async-done | bytes 1179664 | tf_op jit(solution)/shard_map/reduce_scatter | solution.py:253
  911.8 173.2 %reduce-scatter.25.cloned.1.call-done = f32[64,2304]{1,0:T(8,128)} async-done(((f32[1024,2304]{1,0:T(8,128)}), f32[64,2304]{1,0:T(8,128)}) %reduce-scatter.25.cloned.1.call-update) | async-done | bytes 589840
  1085.0 82.2 %reduce-scatter.21.cloned.1.call-done = f32[64,512]{1,0:T(8,128)} async-done(((f32[1024,512]{1,0:T(8,128)}), f32[64,512]{1,0:T(8,128)}) %reduce-scatter.21.cloned.1.call-update) | async-done | bytes 131088 | tf_op jit(solution)/shard_map/reduce_scatter | solution.py:252
  1167.2 136.3 %reduce-scatter.19.cloned.1.call-done = f32[64,3,512]{2,0,1:T(8,128)} async-done(((f32[1024,3,512]{2,0,1:T(8,128)}), f32[64,3,512]{2,0,1:T(8,128)}) %reduce-scatter.19.cloned.1.call-update) | async-done | bytes 393232 | tf_op jit(solution)/shard_map/reduce_scatter | solution.py:251
  (106 shorter events, 43.5 us)
Async XLA Ops:
  7.2 22.7 %all-gather.9.cloned.1.call-start = ((), (), s32[]{:S(2)}) async-start(), calls=%async_computation.8 | async-start | bytes 6291456 | tf_op jit(solution)/shard_map/all_gather | solution.py:184
  7.2 7.7 copy-start.24
  13.4 88.1 %all-gather.11.cloned.1.call-start = ((), (), s32[]{:S(2)}) async-start(), calls=%async_computation.9 | async-start | bytes 3342336 | tf_op jit(solution)/shard_map/all_gather | solution.py:176
  14.1 144.5 %all-gather.13.cloned.1.call-start = ((), (), s32[]{:S(2)}) async-start(), calls=%async_computation.10 | async-start | bytes 1114112 | tf_op jit(solution)/shard_map/all_gather | solution.py:177
  14.9 167.0 %reduce-scatter.11.cloned.1.call-start = ((), (), s32[]{:S(2)}) async-start(), calls=%async_computation.11 | async-start | bytes 12582912 | tf_op jit(solution)/shard_map/reduce_scatter | solution.py:187
  15.0 97.0 %copy-start.18 = (f32[1,512]{1,0:T(1,128)}, f32[1,512]{1,0:T(1,128)S(1)}, u32[]{:S(2)}) copy-start(f32[1,512]{1,0:T(1,128)S(1)} %get-tuple-element.46) | copy-start | bytes 6148
  15.0 97.0 %copy-start.20 = (f32[1,512]{1,0:T(1,128)}, f32[1,512]{1,0:T(1,128)S(1)}, u32[]{:S(2)}) copy-start(f32[1,512]{1,0:T(1,128)S(1)} %get-tuple-element.47) | copy-start | bytes 6148
  15.0 97.0 %copy-start.22 = (f32[1,512]{1,0:T(1,128)}, f32[1,512]{1,0:T(1,128)S(1)}, u32[]{:S(2)}) copy-start(f32[1,512]{1,0:T(1,128)S(1)} %get-tuple-element.48) | copy-start | bytes 6148
  111.9 5.1 copy-start.6
  166.1 15.8 %copy-start.3 = (bf16[1024,1024]{1,0:T(8,128)(2,1)S(1)}, bf16[1024,1024]{1,0:T(8,128)(2,1)}, u32[]{:S(2)}) copy-start(bf16[1024,1024]{1,0:T(8,128)(2,1)} %param.9) | copy-start | bytes 6291460
  166.2 142.9 %all-gather.17.cloned.1.call-start = ((), (), s32[]{:S(2)}) async-start(), calls=%async_computation.13 | async-start | bytes 10027008 | tf_op jit(solution)/shard_map/all_gather | solution.py:178
  168.1 18.6 %copy-start.14 = (f32[1024]{0:T(1024)S(1)}, f32[1024]{0:T(1024)}, u32[]{:S(2)}) copy-start(f32[1024]{0:T(1024)} %param.14) | copy-start | bytes 12292
  168.1 154.4 %all-gather.15.cloned.1.call-start = ((), (), s32[]{:S(2)}) async-start(), calls=%async_computation.12 | async-start | bytes 6291456 | tf_op jit(solution)/shard_map/all_gather | solution.py:210
  188.5 162.1 %all-gather.21.cloned.1.call-start = ((), (), s32[]{:S(2)}) async-start(), calls=%async_computation.16 | async-start | bytes 6291456 | tf_op jit(solution)/shard_map/all_gather | solution.py:211
  189.2 234.6 %all-gather.19.cloned.1.call-start = ((), (), s32[]{:S(2)}) async-start(), calls=%async_computation.14 | async-start | bytes 5013504 | tf_op jit(solution)/shard_map/all_gather | solution.py:179
  190.0 322.5 %reduce-scatter.15.cloned.1.call-start = ((), (), s32[]{:S(2)}) async-start(), calls=%async_computation.17 | async-start | bytes 12582912 | tf_op jit(solution)/shard_map/reduce_scatter | solution.py:223
  496.8 20.3 %copy-start.9 = (bf16[1024,1024]{1,0:T(8,128)(2,1)S(1)}, bf16[1024,1024]{1,0:T(8,128)(2,1)}, u32[]{:S(2)}) copy-start(bf16[1024,1024]{1,0:T(8,128)(2,1)} %param.17) | copy-start | bytes 6291460
  496.9 39.1 %all-gather.23.cloned.1.call-start = ((), (), s32[]{:S(2)}) async-start(), calls=%async_computation.18 | async-start | bytes 6291456 | tf_op jit(solution)/shard_map/all_gather | solution.py:195
  512.4 4.7 copy-start.1
  512.4 5.9 copy-start.5
  518.4 17.6 %copy-start.12 = (bf16[1024,512]{1,0:T(8,128)(2,1)S(1)}, bf16[1024,512]{1,0:T(8,128)(2,1)}, u32[]{:S(2)}) copy-start(bf16[1024,512]{1,0:T(8,128)(2,1)} %all-gather.13.cloned.1.call-done) | copy-start | bytes 3145732
  520.9 144.4 %reduce-scatter.17.cloned.1.call-start = ((), (), s32[]{:S(2)}) async-start(), calls=%async_computation.19 | async-start | bytes 12582912 | tf_op jit(solution)/shard_map/reduce_scatter | solution.py:198
  536.0 9.7 copy-start.8
  545.7 7.5 copy-start.19
  545.7 7.5 copy-start.21
  545.7 7.5 copy-start.23
  559.8 7.8 copy-start.25
  576.5 139.1 %reduce-scatter.13.cloned.1.call-start = ((), (), s32[]{:S(2)}) async-start(), calls=%async_computation.15 | async-start | bytes 12582912 | tf_op jit(solution)/shard_map/reduce_scatter | solution.py:215
  592.9 315.7 %reduce-scatter.23.cloned.1.call-start = ((), (), s32[]{:S(2)}) async-start(), calls=%async_computation.22 | async-start | bytes 20054016 | tf_op jit(solution)/shard_map/reduce_scatter | solution.py:253
  620.2 464.8 %reduce-scatter.25.cloned.1.call-start = ((), (), s32[]{:S(2)}) async-start(), calls=%async_computation.23 | async-start | bytes 10027008
  646.5 520.7 %reduce-scatter.21.cloned.1.call-start = ((), (), s32[]{:S(2)}) async-start(), calls=%async_computation.21 | async-start | bytes 2228224 | tf_op jit(solution)/shard_map/reduce_scatter | solution.py:252
  653.1 650.3 %reduce-scatter.19.cloned.1.call-start = ((), (), s32[]{:S(2)}) async-start(), calls=%async_computation.20 | async-start | bytes 6684672 | tf_op jit(solution)/shard_map/reduce_scatter | solution.py:251
  (10 other events, 18.2 us)
Sparse Core Ops, SparseCore 0:
  13.5 16.3 all-gather.8
  32.7 68.7 all-gather.10
  104.2 54.3 all-gather.12
  166.3 15.5 reduce-scatter.10
  185.4 123.6 all-gather.16
  310.6 11.8 all-gather.14
  324.1 14.8 all-gather.20
  342.1 81.6 all-gather.18
  497.0 15.4 reduce-scatter.14
  521.0 14.9 all-gather.22
  576.6 17.9 reduce-scatter.16
  596.8 18.0 reduce-scatter.12
  620.7 287.8 reduce-scatter.22
  914.7 170.2 reduce-scatter.24
  1087.8 79.3 reduce-scatter.20
  1170.0 133.4 reduce-scatter.18
where the time goes:
time: 1320 us; the launch traced here: 1310 us
  waiting for transfers between devices  950 us (72%)
  matrix products  215 us (16%)
  other arithmetic  55.8 us (4%)
  blocking collectives  44.9 us (3%)
  local copies, waits for them, and re-layouts  28.4 us (2%)
  between operations  14.5 us (1%)
    reduce_scatter x1, waiting for transfers between devices, per_device(): lax.psum_scatter(gate_up_share, 'dp', scatter_dimension=0, tiled=True)  182 us
    unnamed x17, waiting for transfers between devices  176 us
    reduce_scatter x1, waiting for transfers between devices, per_device(): lax.psum_scatter(in_share, 'dp', scatter_dimension=0, tiled=True)  136 us
    all_gather x1, waiting for transfers between devices, per_device(): lax.all_gather(gate_up_weight, 'dp', axis=0, tiled=True)  119 us
    reduce_scatter x1, waiting for transfers between devices, per_device(): lax.psum_scatter(out_share, 'dp', scatter_dimension=0, tiled=True)  82.2 us
    all_gather x1, waiting for transfers between devices, per_device(): lax.all_gather(down_weight, 'dp', axis=0, tiled=True)  73.3 us
    all_gather x1, waiting for transfers between devices, per_device(): lax.all_gather(in_weight, 'dp', axis=0, tiled=True)  71.6 us
    psum x1, blocking collectives, per_device(): lax.psum((gain_grads[0], gain_grads[1], kernel_full), ('dp', 'tensor'))  44.9 us
  transfers between devices with their start and end apart: 16, of which 13 were waited for; matrix products, arithmetic and copies ran while one was open for 12% of the time, Pallas kernels for 0%

commit v1 on v0

--- a/solution.py
+++ b/solution.py
@@ -272,9 +272,211 @@
     )
 
 
+def exchange(values):
+    return lax.ppermute(values, "tensor", [(0, 1), (1, 0)])
+
+
+def across(values, bit):
+    return lax.ppermute(values, "dp", [(place, place ^ bit) for place in range(16)])
+
+
+def line_step(values, first, last, shift):
+    return lax.ppermute(
+        values,
+        "dp",
+        [(place, place + 4 * shift) for place in range(16) if first <= place // 4 <= last],
+    )
+
+
+def place_bits():
+    place = lax.axis_index("dp")
+    return place // 4, (place // 2) % 2, place % 2
+
+
+def gather_line(values, axis):
+    upward, downward, ups, downs = values, values, [], []
+    for step in range(3):
+        upward = line_step(upward, step, 2, 1)
+        downward = line_step(downward, 1, 3 - step, -1)
+        ups.append(upward)
+        downs.append(downward)
+    line = jnp.stack(ups[::-1] + [values] + downs, axis)
+    return lax.dynamic_slice_in_dim(line, 3 - place_bits()[0], 4, axis)
+
+
+def gather_pair(values, bit, axis):
+    other = across(values, bit)
+    own_bit = place_bits()[2 if bit == 1 else 1]
+    return jnp.where(
+        own_bit == 0, jnp.stack([values, other], axis), jnp.stack([other, values], axis)
+    )
+
+
+def add_wide(first, second):
+    return first.astype(jnp.float32) + second.astype(jnp.float32)
+
+
+def reduce_pair(values, bit, axis):
+    own_bit = place_bits()[2 if bit == 1 else 1]
+    other = across(lax.dynamic_index_in_dim(values, 1 - own_bit, axis, keepdims=False), bit)
+    own = lax.dynamic_index_in_dim(values, own_bit, axis, keepdims=False)
+    return add_wide(own, other)
+
+
+def reduce_line(values, axis):
+    level = place_bits()[0]
+
+    def part(index):
+        return lax.dynamic_index_in_dim(values, jnp.clip(index, 0, 3), axis, keepdims=False)
+
+    upward, downward = None, None
+    for step in range(3):
+        up_part, down_part = part(3 - step + level), part(step - 3 + level)
+        if step:
+            up_part = add_wide(up_part, upward).astype(jnp.bfloat16)
+            down_part = add_wide(down_part, downward).astype(jnp.bfloat16)
+        upward = line_step(up_part, 0, min(step, 2), 1)
+        downward = line_step(down_part, max(3 - step, 1), 3, -1)
+    return add_wide(part(level), upward) + downward.astype(jnp.float32)
+
+
+def gather_mixer(in_weight, out_weight):
+    kinds = jnp.concatenate([jnp.transpose(in_weight, (1, 0, 2)), out_weight[None]], 0)
+    lines = gather_line(kinds, 1)
+    first = gather_pair(gather_pair(lines[:2], 2, 2), 1, 3)
+    second = gather_pair(gather_pair(lines[2:], 1, 2), 2, 2)
+    rows = 16 * in_weight.shape[0]
+    return first.reshape(2, rows, -1), second.reshape(2, rows, -1)
+
+
+def gather_gate_up(gate_up_weight):
+    lines = gather_line(jnp.transpose(gate_up_weight, (1, 0, 2)), 1)
+    gate = gather_pair(gather_pair(lines[0], 2, 1), 1, 2)
+    up = gather_pair(gather_pair(lines[1], 1, 1), 2, 1)
+    rows = 16 * gate_up_weight.shape[0]
+    return gate.reshape(rows, -1), up.reshape(rows, -1)
+
+
+def gather_down(down_weight):
+    half = down_weight.shape[0] // 2
+    first = gather_pair(gather_pair(down_weight[:half], 2, 0), 1, 1)
+    second = gather_pair(gather_pair(down_weight[half:], 1, 0), 2, 0)
+    lines = gather_line(jnp.concatenate([first, second], 2), 0)
+    return lines.reshape(16 * down_weight.shape[0], -1)
+
+
+def narrow(values):
+    return values.astype(jnp.bfloat16)
+
+
+def scatter_first(grad):
+    parts = grad.reshape(4, 2, 2, grad.shape[0] // 16, grad.shape[1])
+    return reduce_line(narrow(reduce_pair(narrow(reduce_pair(parts, 1, 2)), 2, 1)), 0)
+
+
+def scatter_second(grad):
+    parts = grad.reshape(4, 2, 2, grad.shape[0] // 16, grad.shape[1])
+    return reduce_line(narrow(reduce_pair(narrow(reduce_pair(parts, 2, 1)), 1, 1)), 0)
+
+
+def scatter_down(grad):
+    rows = grad.shape[0] // 16
+    parts = narrow(reduce_line(grad.reshape(4, 2, 2, rows, grad.shape[1]), 0))
+    first, second = parts[:, :, : rows // 2], parts[:, :, rows // 2 :]
+    first = reduce_pair(narrow(reduce_pair(first, 1, 1)), 2, 0)
+    second = reduce_pair(narrow(reduce_pair(second, 2, 0)), 1, 0)
+    return jnp.concatenate([first, second], 0)
+
+
+def sum_all(values):
+    for bit in (1, 2, 4, 8):
+        values = values + across(values, bit)
+    return values
+
+
+def per_device_pairs(
+    tokens,
+    norm_gain1,
+    in_weight,
+    conv_kernel,
+    out_weight,
+    norm_gain2,
+    gate_up_weight,
+    down_weight,
+    out_grad,
+):
+    rows = tokens.shape[0]
+    dot = lambda spec, a, b: jnp.einsum(spec, a, b, preferred_element_type=jnp.float32)
+    collect = lambda values: jnp.concatenate([values, exchange(values)], 0)
+    merge = lambda values: values[:rows] + exchange(narrow(values[rows:])).astype(jnp.float32)
+    kernel = conv_kernel.astype(jnp.float32)
+    (w_b, w_c), (w_x, w_out) = gather_mixer(in_weight, out_weight)
+    w_down = gather_down(down_weight)
+    w_gate, w_up = gather_gate_up(gate_up_weight)
+    group_grad = collect(out_grad)
+    stream = tokens.astype(jnp.float32)
+    normed1, unit1, inverse1 = rms_forward(stream, norm_gain1)
+    group_n1 = collect(narrow(normed1))
+    b_rows, c_rows, x_rows = (dot("td,dc->tc", group_n1, w) for w in (w_b, w_c, w_x))
+    mixed_in = b_rows * x_rows
+    convolved = causal_conv(mixed_in, kernel)
+    gated = narrow(c_rows * convolved)
+    middle = stream + merge(dot("tc,jc->tj", gated, w_out))
+    normed2, unit2, inverse2 = rms_forward(middle, norm_gain2)
+    group_n2 = collect(narrow(normed2))
+    grad_hidden = dot("tj,jf->tf", group_grad, w_down)
+    gate = dot("td,df->tf", group_n2, w_gate)
+    up = dot("td,df->tf", group_n2, w_up)
+    sigm = jax.nn.sigmoid(gate)
+    hidden = narrow(gate * sigm * up)
+    grad_up = narrow(grad_hidden * gate * sigm)
+    grad_gate = narrow(grad_hidden * up * sigm * (1.0 + gate * (1.0 - sigm)))
+    down_final = scatter_down(narrow(dot("tj,tf->jf", group_grad, hidden)))
+    gate_final = scatter_first(narrow(dot("td,tf->df", group_n2, grad_gate)))
+    up_final = scatter_second(narrow(dot("td,tf->df", group_n2, grad_up)))
+    grad_normed2 = merge(
+        dot("tf,df->td", grad_gate, w_gate) + dot("tf,df->td", grad_up, w_up)
+    )
+    result = narrow(middle + merge(dot("tf,jf->tj", hidden, w_down)))
+    grad_rms2, gain_two_grad = rms_backward(grad_normed2, unit2, inverse2, norm_gain2)
+    grad_middle = out_grad.astype(jnp.float32) + grad_rms2
+    group_gm = collect(narrow(grad_middle))
+    grad_gated = dot("tj,jc->tc", group_gm, w_out)
+    out_final = scatter_second(narrow(dot("tj,tc->jc", group_gm, gated)))
+    grad_c = narrow(grad_gated * convolved)
+    grad_mixed, kernel_grad = conv_backward(grad_gated * c_rows, mixed_in, kernel)
+    grad_b, grad_x = narrow(grad_mixed * x_rows), narrow(grad_mixed * b_rows)
+    b_final = scatter_first(narrow(dot("td,tc->dc", group_n1, grad_b)))
+    c_final = scatter_first(narrow(dot("td,tc->dc", group_n1, grad_c)))
+    x_final = scatter_second(narrow(dot("td,tc->dc", group_n1, grad_x)))
+    grad_normed1 = merge(
+        dot("tc,dc->td", grad_b, w_b)
+        + dot("tc,dc->td", grad_c, w_c)
+        + dot("tc,dc->td", grad_x, w_x)
+    )
+    grad_rms1, gain_one_grad = rms_backward(grad_normed1, unit1, inverse1, norm_gain1)
+    input_grad = grad_middle + grad_rms1
+    summed = sum_all(jnp.concatenate([gain_one_grad, gain_two_grad, kernel_grad.reshape(-1)]))
+    width = gain_one_grad.shape[0]
+    gains = summed[: 2 * width]
+    gains = gains + exchange(gains)
+    return (
+        result,
+        input_grad,
+        gains[:width],
+        jnp.stack([b_final, c_final, x_final], 1),
+        summed[2 * width :].reshape(kernel_grad.shape),
+        out_final,
+        gains[width:],
+        jnp.stack([gate_final, up_final], 1),
+        down_final,
+    )
+
+
 def solution(mesh):
+    paired = mesh.shape["dp"] == 16 and mesh.shape["tensor"] == 2
     return jax.shard_map(
-        per_device,
+        per_device_pairs if paired else per_device,
         mesh=mesh,
         in_specs=(
             P(("dp", "tensor"), None),

time: 1320 us -> 735 us (0.56)
  waiting for transfers between devices: 950 us -> 218 us
  starting transfers between devices: 1.03 us -> 181 us
  blocking collectives: 44.9 us -> 0 us
  local copies, waits for them, and re-layouts: 28.4 us -> 64.2 us
  matrix products: 215 us -> 196 us
    reduce_scatter x7 -> x0, waiting for transfers between devices: 430 us -> none  [the longest x1 182 us: per_device(): lax.psum_scatter(gate_up_share, 'dp', scatter_dimension=0, tiled=True)]
    all_gather x8 -> x0, waiting for transfers between devices: 344 us -> none  [the longest x1 119 us: per_device(): lax.all_gather(gate_up_weight, 'dp', axis=0, tiled=True)]
    ppermute x0 -> x101, waiting for transfers between devices: none -> 218 us  [the longest x60 128 us: line_step(): lax.ppermute(values, 'dp', [(place, place + 4 * shift) for place in range...]
    ppermute x0 -> x101, starting transfers between devices: none -> 181 us  [the longest x60 141 us: line_step(): lax.ppermute(values, 'dp', [(place, place + 4 * shift) for place in range...]
    unnamed x17 -> x0, waiting for transfers between devices: 176 us -> none
    psum x1 -> x0, blocking collectives: 44.9 us -> none  [per_device(): lax.psum((gain_grads[0], gain_grads[1], kernel_full), ('dp', 'tensor'))]
    convert_element_type x4 -> x41, other arithmetic: 10.1 us -> 33.7 us  [the longest x20 23.1 us: narrow(): return values.astype(jnp.bfloat16)]
    dot_general x12 -> x21, matrix products: 215 us -> 196 us  [per_device_pairs(): jnp.einsum(spec, a, b, preferred_element_type=jnp.float32)]
  transfers between devices with their start and end apart: 16 -> 101, of which waited for: 13 -> 34; matrix products, arithmetic and copies ran while one was open for 12% -> 33% of each run, Pallas kernels for 0% -> 0%
where the time goes in v1:
time: 735 us; the launch traced here: 728 us
  waiting for transfers between devices  218 us (30%)
  matrix products  196 us (27%)
  starting transfers between devices  181 us (25%)
  other arithmetic  65.4 us (9%)
  local copies, waits for them, and re-layouts  64.2 us (9%)
    dot_general x21, matrix products, per_device_pairs(): jnp.einsum(spec, a, b, preferred_element_type=jnp.float32)  196 us
    ppermute x60, starting transfers between devices, line_step(): lax.ppermute(values, 'dp', [(place, place + 4 * shift) for place in range...  141 us
    ppermute x60, waiting for transfers between devices, line_step(): lax.ppermute(values, 'dp', [(place, place + 4 * shift) for place in range...  128 us
    ppermute x32, waiting for transfers between devices, across(): lax.ppermute(values, 'dp', [(place, place ^ bit) for place in range(16)])  89.9 us
    ppermute x32, starting transfers between devices, across(): lax.ppermute(values, 'dp', [(place, place ^ bit) for place in range(16)])  38.7 us
    unnamed x181, local copies, waits for them, and re-layouts  28.4 us
    convert_element_type x20, other arithmetic, narrow(): return values.astype(jnp.bfloat16)  23.1 us
  transfers between devices with their start and end apart: 101, of which 34 were waited for; matrix products, arithmetic and copies ran while one was open for 33% of the time, Pallas kernels for 0%

profile of v1, /device:TPU:0, one launch (start us, length us, event | category | flops | bytes accessed | tf_op | source)
XLA Modules:
  0.0 728.1 jit_solution(4397901484578662112)
XLA Ops:
  2.8 5.7 collective-permute-start.13
  11.5 5.3 collective-permute-start.1
  39.9 6.9 collective-permute-done.5
  58.9 6.4 collective-permute-done.7
  72.5 14.7 %collective-permute-done.17 = bf16[2,64,2304]{2,1,0:T(8,128)(2,1)S(1)} collective-permute-done((bf16[2,64,2304]{2,1,0:T(8,128)(2,1)S(1)}, bf16[2,64,2304]{2,1,0:T(8,128)(2,1)S(1)}, u32[]{:S(2)}, u32[]{:S(2)}) %collective-permute-start.17) | collective-permute-done | bytes 589856 | tf_op jit(solution)/shard_map/ppermute | solution.py:284
  91.2 37.8 %collective-permute-done.18 = bf16[2,64,2304]{2,1,0:T(8,128)(2,1)S(1)} collective-permute-done((bf16[2,64,2304]{2,1,0:T(8,128)(2,1)S(1)}, bf16[2,64,2304]{2,1,0:T(8,128)(2,1)S(1)}, u32[]{:S(2)}, u32[]{:S(2)}) %collective-permute-start.18) | collective-permute-done | bytes 589856 | tf_op jit(solution)/shard_map/ppermute | solution.py:284
  136.8 15.8 %collective-permute-done.10 = bf16[2,4,2,64,512]{4,3,1,0,2:T(8,128)(2,1)S(1)} collective-permute-done((bf16[2,4,2,64,512]{4,3,1,0,2:T(8,128)(2,1)S(1)}, bf16[2,4,2,64,512]{4,3,1,0,2:T(8,128)(2,1)S(1)}, u32[]{:S(2)}, u32[]{:S(2)}) %collective-permute-start.10) | collective-permute-done | bytes 1048608 | tf_op jit(solution)/shard_map/ppermute | solution.py:280
  165.8 7.7 %fusion.17 = (bf16[2048,512]{1,0:T(8,128)(2,1)S(1)}, f32[2048,512]{1,0:T(8,128)}) fusion(f32[2,1024,512]{2,1,0:T(8,128)S(1)} %multiply_add_fusion.2, bf16[1024,512]{1,0:T(8,128)(2,1)} %bitcast.469, bf16[1024,1024]{1,0:T(8,128)(2,1)} %copy-done.35, bf16[1024,1024]{1,0:T(8,128)(2,1)S(1)} %copy-done.19), kind=kOutput, calls=%fused_computation.47 | convolution fusion | flops 2157969408 | bytes 15728640 | tf_op jit(solution)/shard_map/td,dc->tc/dot_general | solution.py:409
  198.4 10.3 %collective-permute-done.32 = bf16[2,2,64,2304]{3,2,1,0:T(8,128)(2,1)S(1)} collective-permute-done((bf16[2,2,64,2304]{3,2,1,0:T(8,128)(2,1)}, bf16[2,2,64,2304]{3,2,1,0:T(8,128)(2,1)S(1)}, u32[]{:S(2)}, u32[]{:S(2)}) %collective-permute-start.32) | collective-permute-done | bytes 1179680 | tf_op jit(solution)/shard_map/ppermute | solution.py:284
  218.5 13.2 %fusion.92 = f32[2048,2304]{1,0:T(8,128)} fusion(bf16[2048,1024]{1,0:T(8,128)(2,1)S(1)} %copy-done.41, bf16[1024,2304]{1,0:T(8,128)(2,1)S(1)} %bitcast.443), kind=kOutput, calls=%fused_computation.302 | convolution fusion | flops 9663676416 | bytes 27787264 | tf_op jit(solution)/shard_map/tj,jf->tf/dot_general | solution.py:409
  245.1 13.2 %fusion.78 = f32[2048,2304]{1,0:T(8,128)} fusion(bf16[1024,2304]{1,0:T(8,128)(2,1)S(1)} %bitcast.441, bf16[1024,1024]{1,0:T(8,128)(2,1)S(1)} %collective-permute-done.12, bf16[1024,1024]{1,0:T(8,128)(2,1)S(1)} %multiply_convert_fusion.3), kind=kOutput, calls=%fused_computation.288 | convolution fusion | flops 9672065024 | bytes 27787264 | tf_op jit(solution)/shard_map/td,df->tf/dot_general | solution.py:409
  258.3 30.5 %multiply_convert_fusion.1 = (bf16[2048,2304]{1,0:T(8,128)(2,1)}, bf16[2048,2304]{1,0:T(8,128)(2,1)}, bf16[2048,2304]{1,0:T(8,128)(2,1)}) fusion(f32[2048,2304]{1,0:T(8,128)} %fusion.92, f32[2048,2304]{1,0:T(8,128)} %fusion.78, bf16[1024,2304]{1,0:T(8,128)(2,1)} %bitcast.445, bf16[1024,1024]{1,0:T(8,128)(2,1)} %copy-done.66, ...), kind=kOutput, calls=%fused_computation.1 | convolution fusion | flops 9747562496 | bytes 74973184 | tf_op jit(solution)/shard_map/td,df->tf/dot_general | solution.py:409
  288.8 14.4 %convolution_convert_fusion = bf16[1024,2304]{1,0:T(8,128)(2,1)S(1)} fusion(bf16[2048,1024]{1,0:T(8,128)(2,1)} %copy-done.40, bf16[2048,2304]{1,0:T(8,128)(2,1)} %get-tuple-element.30), kind=kOutput, calls=%fused_computation.12 | convolution fusion | flops 9666035712 | bytes 18350080 | tf_op jit(solution)/shard_map/tj,tf->jf/dot_general | solution.py:409
  303.2 16.2 %fusion.91 = f32[2048,1024]{1,0:T(8,128)} fusion(bf16[2048,2304]{1,0:T(8,128)(2,1)S(1)} %copy-done.71, bf16[1024,2304]{1,0:T(8,128)(2,1)} %bitcast.444), kind=kOutput, calls=%fused_computation.301 | convolution fusion | flops 9663676416 | bytes 22544384 | tf_op jit(solution)/shard_map/tf,jf->tj/dot_general | solution.py:409
  320.6 5.4 collective-permute-start.91
  327.7 12.8 %convolution_convert_fusion.2 = bf16[1024,2304]{1,0:T(8,128)(2,1)S(1)} fusion(bf16[2048,2304]{1,0:T(8,128)(2,1)} %get-tuple-element.29, bf16[1024,1024]{1,0:T(8,128)(2,1)S(1)} %copy-done.67, bf16[1024,1024]{1,0:T(8,128)(2,1)S(1)} %multiply_convert_fusion.3), kind=kOutput, calls=%fused_computation.14 | convolution fusion | flops 9674424320 | bytes 18350080 | tf_op jit(solution)/shard_map/td,tf->df/dot_general | solution.py:409
  348.8 12.9 %fusion.93 = f32[2048,1024]{1,0:T(8,128)} fusion(bf16[2048,2304]{1,0:T(8,128)(2,1)S(1)} %bitcast.495, bf16[1024,2304]{1,0:T(8,128)(2,1)S(1)} %bitcast.442), kind=kOutput, calls=%fused_computation.303 | convolution fusion | flops 9663676416 | bytes 22544384 | tf_op jit(solution)/shard_map/tf,df->td/dot_general | solution.py:409
  361.7 15.1 %convolution_add_fusion = f32[2048,1024]{1,0:T(8,128)S(1)} fusion(f32[2048,1024]{1,0:T(8,128)} %fusion.93, bf16[2048,2304]{1,0:T(8,128)(2,1)} %get-tuple-element.29, bf16[1024,2304]{1,0:T(8,128)(2,1)} %bitcast.446), kind=kOutput, calls=%fused_computation.61 | convolution fusion | flops 9665773568 | bytes 30932992 | tf_op jit(solution)/shard_map/tf,df->td/dot_general | solution.py:409
  379.9 12.9 %convolution_convert_fusion.1 = bf16[1024,2304]{1,0:T(8,128)(2,1)S(1)} fusion(bf16[2048,2304]{1,0:T(8,128)(2,1)} %get-tuple-element.31, bf16[1024,1024]{1,0:T(8,128)(2,1)S(1)} %copy-done.68, bf16[1024,1024]{1,0:T(8,128)(2,1)S(1)} %copy-done.32), kind=kOutput, calls=%fused_computation.13 | convolution fusion | flops 9674424320 | bytes 18350080 | tf_op jit(solution)/shard_map/td,tf->df/dot_general | solution.py:409
  402.9 6.3 fusion.83
  409.4 16.7 %collective-permute-done.92 = bf16[2,2,64,2304]{3,2,1,0:T(8,128)(2,1)} collective-permute-done((bf16[2,2,64,2304]{3,2,1,0:T(8,128)(2,1)}, bf16[2,2,64,2304]{3,2,1,0:T(8,128)(2,1)}, u32[]{:S(2)}, u32[]{:S(2)}) %collective-permute-start.92) | collective-permute-done | bytes 1179680 | tf_op jit(solution)/shard_map/ppermute | solution.py:284
  430.0 6.1 collective-permute-start.93
  439.3 9.7 %collective-permute-done.83 = bf16[4,2,64,2304]{3,2,0,1:T(8,128)(2,1)S(1)} collective-permute-done((bf16[4,2,64,2304]{3,2,0,1:T(8,128)(2,1)}, bf16[4,2,64,2304]{3,2,0,1:T(8,128)(2,1)S(1)}, u32[]{:S(2)}, u32[]{:S(2)}) %collective-permute-start.83) | collective-permute-done | bytes 2359328 | tf_op jit(solution)/shard_map/ppermute | solution.py:280
  453.4 20.5 %collective-permute-done.76 = bf16[4,64,2304]{2,1,0:T(8,128)(2,1)S(1)} collective-permute-done((bf16[4,64,2304]{2,1,0:T(8,128)(2,1)S(1)}, bf16[4,64,2304]{2,1,0:T(8,128)(2,1)S(1)}, u32[]{:S(2)}, u32[]{:S(2)}) %collective-permute-start.76) | collective-permute-done | bytes 1179680 | tf_op jit(solution)/shard_map/ppermute | solution.py:280
  486.6 5.7 collective-permute-done.85
  517.8 8.4 %multiply_reduce_fusion.2 = (f32[512]{0:T(512)S(1)}, f32[512]{0:T(512)S(1)}, f32[2048,512]{1,0:T(8,128)S(1)}, f32[2048,512]{1,0:T(8,128)}) fusion(f32[2,1024,512]{2,1,0:T(8,128)S(1)} %bitcast.424, f32[2048,512]{1,0:T(8,128)} %get-tuple-element.105, bf16[1024,512]{1,0:T(8,128)(2,1)S(1)} %bitcast.466, bf16[1024,1024]{1,0:T(8,128)(2,1)S(1)} %collective-permute-done.36, ...), kind=kOutput, calls=%fused_computation.51 | convolution fusion | flops 2161114112 | bytes 22024192 | tf_op jit(solution)/shard_map/tj,jc->tc/dot_general | solution.py:409
  534.0 7.7 %fusion.95 = f32[2048,1024]{1,0:T(8,128)} fusion(bf16[2048,512]{1,0:T(8,128)(2,1)} %get-tuple-element.107, bf16[1024,512]{1,0:T(8,128)(2,1)} %bitcast.470), kind=kOutput, calls=%fused_computation.305 | convolution fusion | flops 2147483648 | bytes 11534336 | tf_op jit(solution)/shard_map/tc,dc->td/dot_general | solution.py:409
  555.7 5.8 add_add_fusion
  594.5 5.6 collective-permute-done.90
  607.4 10.0 %collective-permute-done.68 = bf16[4,64,512]{2,1,0:T(8,128)(2,1)S(1)} collective-permute-done((bf16[4,64,512]{2,1,0:T(8,128)(2,1)S(1)}, bf16[4,64,512]{2,1,0:T(8,128)(2,1)S(1)}, u32[]{:S(2)}, u32[]{:S(2)}) %collective-permute-start.68) | collective-permute-done | bytes 262176 | tf_op jit(solution)/shard_map/ppermute | solution.py:280
  619.4 5.9 collective-permute-done.52
  685.5 11.3 %collective-permute-start.63 = (bf16[64,512]{1,0:T(8,128)(2,1)S(1)}, bf16[64,512]{1,0:T(8,128)(2,1)S(1)}, u32[]{:S(2)}, u32[]{:S(2)}) collective-permute-start(bf16[64,512]{1,0:T(8,128)(2,1)S(1)} %get-tuple-element.93), channel_id=1, source_target_pairs={{0,8},{2,10},{4,12},{6,14},{8,16},{10,18},{12,20},{14,22},{16,24},... | collective-permute-start | bytes 196616 | tf_op jit(solution)/shard_map/ppermute | solution.py:284
  (522 shorter events, 347.9 us)
Async XLA Ops:
  2.8 44.9 %collective-permute-start.13 = (bf16[2,64,2304]{2,1,0:T(8,128)(2,1)}, bf16[2,64,2304]{2,1,0:T(8,128)(2,1)}, u32[]{:S(2)}, u32[]{:S(2)}) collective-permute-start(bf16[2,64,2304]{2,1,0:T(8,128)(2,1)} %bitcast.422), channel_id=1, source_target_pairs={{0,8},{2,10},{4,12},{6,14},{8,16},{10,18},{12,20},{14,22},{16,24},... | collective-permute-start | bytes 1769480 | tf_op jit(solution)/shard_map/ppermute | solution.py:284
  8.5 57.0 %collective-permute-start.16 = (bf16[2,64,2304]{2,1,0:T(8,128)(2,1)}, bf16[2,64,2304]{2,1,0:T(8,128)(2,1)S(1)}, u32[]{:S(2)}, u32[]{:S(2)}) collective-permute-start(bf16[2,64,2304]{2,1,0:T(8,128)(2,1)} %bitcast.422), channel_id=1, source_target_pairs={{8,0},{10,2},{12,4},{14,6},{16,8},{18,10},{20,12},{22,14},{24,16},... | collective-permute-start | bytes 1769480 | tf_op jit(solution)/shard_map/ppermute | solution.py:284
  33.2 101.9 %collective-permute-start.34 = (bf16[1024,1024]{1,0:T(8,128)(2,1)S(1)}, bf16[1024,1024]{1,0:T(8,128)(2,1)S(1)}, u32[]{:S(2)}, u32[]{:S(2)}) collective-permute-start(bf16[1024,1024]{1,0:T(8,128)(2,1)S(1)} %copy-done.17), channel_id=1, source_target_pairs={{0,1},{1,0},{2,3},{3,2},{4,5},{5,4},{6,7},{7,6},{8,9},{9,8},{10,11... | collective-permute-start | bytes 6291464 | tf_op jit(solution)/shard_map/ppermute | solution.py:276
  65.4 91.6 %collective-permute-start = (bf16[1024,1024]{1,0:T(8,128)(2,1)S(1)}, bf16[1024,1024]{1,0:T(8,128)(2,1)S(1)}, u32[]{:S(2)}, u32[]{:S(2)}) collective-permute-start(bf16[1024,1024]{1,0:T(8,128)(2,1)S(1)} %copy-done.19), channel_id=1, source_target_pairs={{0,1},{1,0},{2,3},{3,2},{4,5},{5,4},{6,7},{7,6},{8,9},{9,8},{10,11... | collective-permute-start | bytes 6291464 | tf_op jit(solution)/shard_map/ppermute | solution.py:276
  65.5 64.4 %collective-permute-start.27 = (bf16[2,2,64,2304]{3,2,1,0:T(8,128)(2,1)S(1)}, bf16[2,2,64,2304]{3,2,1,0:T(8,128)(2,1)}, u32[]{:S(2)}, u32[]{:S(2)}) collective-permute-start(bf16[2,2,64,2304]{3,2,1,0:T(8,128)(2,1)S(1)} %pad_maximum_fusion.7), channel_id=1, source_target_pairs={{0,8},{2,10},{4,12},{6,14},{8,16},{10,18},{12,20},{14,22},{16,24},... | collective-permute-start | bytes 3538952 | tf_op jit(solution)/shard_map/ppermute | solution.py:284
  87.2 46.2 %collective-permute-start.30 = (bf16[2,2,64,2304]{3,2,1,0:T(8,128)(2,1)S(1)}, bf16[2,2,64,2304]{3,2,1,0:T(8,128)(2,1)}, u32[]{:S(2)}, u32[]{:S(2)}) collective-permute-start(bf16[2,2,64,2304]{3,2,1,0:T(8,128)(2,1)S(1)} %pad_maximum_fusion.7), channel_id=1, source_target_pairs={{8,0},{10,2},{12,4},{14,6},{16,8},{18,10},{20,12},{22,14},{24,16},... | collective-permute-start | bytes 3538952 | tf_op jit(solution)/shard_map/ppermute | solution.py:284
  88.5 40.5 %collective-permute-start.18 = (bf16[2,64,2304]{2,1,0:T(8,128)(2,1)S(1)}, bf16[2,64,2304]{2,1,0:T(8,128)(2,1)S(1)}, u32[]{:S(2)}, u32[]{:S(2)}) collective-permute-start(bf16[2,64,2304]{2,1,0:T(8,128)(2,1)S(1)} %collective-permute-done.17), channel_id=1, source_target_pairs={{8,0},{10,2},{12,4},{14,6},{9,1},{11,3},{13,5},{15,7}} | collective-permute-start | bytes 1769480 | tf_op jit(solution)/shard_map/ppermute | solution.py:284
  133.4 44.0 %collective-permute-start.28 = (bf16[2,2,64,2304]{3,2,1,0:T(8,128)(2,1)}, bf16[2,2,64,2304]{3,2,1,0:T(8,128)(2,1)}, u32[]{:S(2)}, u32[]{:S(2)}) collective-permute-start(bf16[2,2,64,2304]{3,2,1,0:T(8,128)(2,1)} %collective-permute-done.27), channel_id=1, source_target_pairs={{8,16},{10,18},{12,20},{14,22},{16,24},{18,26},{20,28},{22,30},{9,... | collective-permute-start | bytes 3538952 | tf_op jit(solution)/shard_map/ppermute | solution.py:284
  135.1 43.1 %collective-permute-start.31 = (bf16[2,2,64,2304]{3,2,1,0:T(8,128)(2,1)}, bf16[2,2,64,2304]{3,2,1,0:T(8,128)(2,1)}, u32[]{:S(2)}, u32[]{:S(2)}) collective-permute-start(bf16[2,2,64,2304]{3,2,1,0:T(8,128)(2,1)} %collective-permute-done.30), channel_id=1, source_target_pairs={{8,0},{10,2},{12,4},{14,6},{16,8},{18,10},{20,12},{22,14},{9,1},{1... | collective-permute-start | bytes 3538952 | tf_op jit(solution)/shard_map/ppermute | solution.py:284
  154.7 28.7 %collective-permute-start.19 = (bf16[4,64,2304]{2,1,0:T(8,128)(2,1)}, bf16[4,64,2304]{2,1,0:T(8,128)(2,1)S(1)}, u32[]{:S(2)}, u32[]{:S(2)}) collective-permute-start(bf16[4,64,2304]{2,1,0:T(8,128)(2,1)} %get-tuple-element.46), channel_id=1, source_target_pairs={{0,4},{2,6},{4,0},{6,2},{8,12},{10,14},{12,8},{14,10},{16,20},{18,... | collective-permute-start | bytes 3538952 | tf_op jit(solution)/shard_map/ppermute | solution.py:280
  177.4 35.2 %collective-permute-start.11 = (bf16[1024,1024]{1,0:T(8,128)(2,1)S(1)}, bf16[1024,1024]{1,0:T(8,128)(2,1)S(1)}, u32[]{:S(2)}, u32[]{:S(2)}) collective-permute-start(bf16[1024,1024]{1,0:T(8,128)(2,1)S(1)} %slice.198), channel_id=1, source_target_pairs={{0,1},{1,0},{2,3},{3,2},{4,5},{5,4},{6,7},{7,6},{8,9},{9,8},{10,11... | collective-permute-start | bytes 6291464 | tf_op jit(solution)/shard_map/ppermute | solution.py:276
  178.2 30.5 %collective-permute-start.32 = (bf16[2,2,64,2304]{3,2,1,0:T(8,128)(2,1)}, bf16[2,2,64,2304]{3,2,1,0:T(8,128)(2,1)S(1)}, u32[]{:S(2)}, u32[]{:S(2)}) collective-permute-start(bf16[2,2,64,2304]{3,2,1,0:T(8,128)(2,1)} %collective-permute-done.31), channel_id=1, source_target_pairs={{8,0},{10,2},{12,4},{14,6},{9,1},{11,3},{13,5},{15,7}} | collective-permute-start | bytes 3538952 | tf_op jit(solution)/shard_map/ppermute | solution.py:284
  182.2 53.3 %collective-permute-start.22 = (bf16[4,2,64,2304]{3,2,0,1:T(8,128)(2,1)}, bf16[4,2,64,2304]{3,2,0,1:T(8,128)(2,1)}, u32[]{:S(2)}, u32[]{:S(2)}) collective-permute-start(bf16[4,2,64,2304]{3,2,0,1:T(8,128)(2,1)} %maximum_select_fusion.5), channel_id=1, source_target_pairs={{0,4},{2,6},{4,0},{6,2},{8,12},{10,14},{12,8},{14,10},{16,20},{18,... | collective-permute-start | bytes 7077896 | tf_op jit(solution)/shard_map/ppermute | solution.py:280
  185.1 54.1 %collective-permute-start.20 = (bf16[4,2,64,2304]{3,2,0,1:T(8,128)(2,1)}, bf16[4,2,64,2304]{3,2,0,1:T(8,128)(2,1)}, u32[]{:S(2)}, u32[]{:S(2)}) collective-permute-start(bf16[4,2,64,2304]{3,2,0,1:T(8,128)(2,1)} %maximum_select_fusion.3), channel_id=1, source_target_pairs={{0,2},{2,0},{4,6},{6,4},{8,10},{10,8},{12,14},{14,12},{16,18},{18,... | collective-permute-start | bytes 7077896 | tf_op jit(solution)/shard_map/ppermute | solution.py:280
  216.8 28.2 %collective-permute-start.12 = (bf16[1024,1024]{1,0:T(8,128)(2,1)S(1)}, bf16[1024,1024]{1,0:T(8,128)(2,1)S(1)}, u32[]{:S(2)}, u32[]{:S(2)}) collective-permute-start(bf16[1024,1024]{1,0:T(8,128)(2,1)S(1)} %multiply_convert_fusion.3), channel_id=1, source_target_pairs={{0,1},{1,0},{2,3},{3,2},{4,5},{5,4},{6,7},{7,6},{8,9},{9,8},{10,11... | collective-permute-start | bytes 6291464 | tf_op jit(solution)/shard_map/ppermute | solution.py:276
  320.6 74.2 %collective-permute-start.91 = (bf16[2,2,64,2304]{3,2,1,0:T(8,128)(2,1)}, bf16[2,2,64,2304]{3,2,1,0:T(8,128)(2,1)}, u32[]{:S(2)}, u32[]{:S(2)}) collective-permute-start(bf16[2,2,64,2304]{3,2,1,0:T(8,128)(2,1)} %get-tuple-element.34), channel_id=1, source_target_pairs={{0,8},{2,10},{4,12},{6,14},{1,9},{3,11},{5,13},{7,15}} | collective-permute-start | bytes 3538952 | tf_op jit(solution)/shard_map/ppermute | solution.py:284
  326.0 83.5 %collective-permute-start.94 = (bf16[2,2,64,2304]{3,2,1,0:T(8,128)(2,1)S(1)}, bf16[2,2,64,2304]{3,2,1,0:T(8,128)(2,1)}, u32[]{:S(2)}, u32[]{:S(2)}) collective-permute-start(bf16[2,2,64,2304]{3,2,1,0:T(8,128)(2,1)S(1)} %get-tuple-element.35), channel_id=1, source_target_pairs={{24,16},{26,18},{28,20},{30,22},{25,17},{27,19},{29,21},{31,23}} | collective-permute-start | bytes 3538952 | tf_op jit(solution)/shard_map/ppermute | solution.py:284
  344.0 92.2 %collective-permute-start.75 = (bf16[4,2,64,2304]{3,2,0,1:T(8,128)(2,1)}, bf16[4,2,64,2304]{3,2,0,1:T(8,128)(2,1)}, u32[]{:S(2)}, u32[]{:S(2)}) collective-permute-start(bf16[4,2,64,2304]{3,2,0,1:T(8,128)(2,1)} %bitcast.417), channel_id=1, source_target_pairs={{0,2},{2,0},{4,6},{6,4},{8,10},{10,8},{12,14},{14,12},{16,18},{18,... | collective-permute-start | bytes 7077896 | tf_op jit(solution)/shard_map/ppermute | solution.py:280
  348.8 54.1 %collective-permute-start.33 = (bf16[1024,1024]{1,0:T(8,128)(2,1)}, bf16[1024,1024]{1,0:T(8,128)(2,1)}, u32[]{:S(2)}, u32[]{:S(2)}) collective-permute-start(bf16[1024,1024]{1,0:T(8,128)(2,1)} %slice.197), channel_id=1, source_target_pairs={{0,1},{1,0},{2,3},{3,2},{4,5},{5,4},{6,7},{7,6},{8,9},{9,8},{10,11... | collective-permute-start | bytes 6291464 | tf_op jit(solution)/shard_map/ppermute | solution.py:276
  394.7 54.3 %collective-permute-start.83 = (bf16[4,2,64,2304]{3,2,0,1:T(8,128)(2,1)}, bf16[4,2,64,2304]{3,2,0,1:T(8,128)(2,1)S(1)}, u32[]{:S(2)}, u32[]{:S(2)}) collective-permute-start(bf16[4,2,64,2304]{3,2,0,1:T(8,128)(2,1)} %bitcast.416), channel_id=1, source_target_pairs={{0,4},{2,6},{4,0},{6,2},{8,12},{10,14},{12,8},{14,10},{16,20},{18,... | collective-permute-start | bytes 7077896 | tf_op jit(solution)/shard_map/ppermute | solution.py:280
  398.5 27.6 %collective-permute-start.92 = (bf16[2,2,64,2304]{3,2,1,0:T(8,128)(2,1)}, bf16[2,2,64,2304]{3,2,1,0:T(8,128)(2,1)}, u32[]{:S(2)}, u32[]{:S(2)}) collective-permute-start(bf16[2,2,64,2304]{3,2,1,0:T(8,128)(2,1)} %fusion.23), channel_id=1, source_target_pairs={{0,8},{2,10},{4,12},{6,14},{8,16},{10,18},{12,20},{14,22},{1,9},{3... | collective-permute-start | bytes 3538952 | tf_op jit(solution)/shard_map/ppermute | solution.py:284
  409.2 107.0 %collective-permute-start.36 = (bf16[1024,1024]{1,0:T(8,128)(2,1)}, bf16[1024,1024]{1,0:T(8,128)(2,1)S(1)}, u32[]{:S(2)}, u32[]{:S(2)}) collective-permute-start(bf16[1024,1024]{1,0:T(8,128)(2,1)} %get-tuple-element.25), channel_id=1, source_target_pairs={{0,1},{1,0},{2,3},{3,2},{4,5},{5,4},{6,7},{7,6},{8,9},{9,8},{10,11... | collective-permute-start | bytes 6291464 | tf_op jit(solution)/shard_map/ppermute | solution.py:276
  430.0 150.1 %collective-permute-start.93 = (bf16[2,2,64,2304]{3,2,1,0:T(8,128)(2,1)}, bf16[2,2,64,2304]{3,2,1,0:T(8,128)(2,1)}, u32[]{:S(2)}, u32[]{:S(2)}) collective-permute-start(bf16[2,2,64,2304]{3,2,1,0:T(8,128)(2,1)} %get-tuple-element.32), channel_id=1, source_target_pairs={{0,8},{2,10},{4,12},{6,14},{8,16},{10,18},{12,20},{14,22},{16,24},... | collective-permute-start | bytes 3538952 | tf_op jit(solution)/shard_map/ppermute | solution.py:284
  438.4 35.5 %collective-permute-start.76 = (bf16[4,64,2304]{2,1,0:T(8,128)(2,1)S(1)}, bf16[4,64,2304]{2,1,0:T(8,128)(2,1)S(1)}, u32[]{:S(2)}, u32[]{:S(2)}) collective-permute-start(bf16[4,64,2304]{2,1,0:T(8,128)(2,1)S(1)} %dynamic-slice_bitcast_fusion.3), channel_id=1, source_target_pairs={{0,4},{2,6},{4,0},{6,2},{8,12},{10,14},{12,8},{14,10},{16,20},{18,... | collective-permute-start | bytes 3538952 | tf_op jit(solution)/shard_map/ppermute | solution.py:280
  452.1 129.2 %collective-permute-start.96 = (bf16[2,2,64,2304]{3,2,1,0:T(8,128)(2,1)}, bf16[2,2,64,2304]{3,2,1,0:T(8,128)(2,1)}, u32[]{:S(2)}, u32[]{:S(2)}) collective-permute-start(bf16[2,2,64,2304]{3,2,1,0:T(8,128)(2,1)} %fusion.22), channel_id=1, source_target_pairs={{8,0},{10,2},{12,4},{14,6},{16,8},{18,10},{20,12},{22,14},{24,16},... | collective-permute-start | bytes 3538952 | tf_op jit(solution)/shard_map/ppermute | solution.py:284
  506.9 69.5 %collective-permute-start.81 = (bf16[64,2304]{1,0:T(8,128)(2,1)}, bf16[64,2304]{1,0:T(8,128)(2,1)S(1)}, u32[]{:S(2)}, u32[]{:S(2)}) collective-permute-start(bf16[64,2304]{1,0:T(8,128)(2,1)} %get-tuple-element.58), channel_id=1, source_target_pairs={{16,8},{18,10},{20,12},{22,14},{24,16},{26,18},{28,20},{30,22},{17... | collective-permute-start | bytes 884744 | tf_op jit(solution)/shard_map/ppermute | solution.py:284
  510.1 75.0 %collective-permute-start.79 = (bf16[64,2304]{1,0:T(8,128)(2,1)}, bf16[64,2304]{1,0:T(8,128)(2,1)}, u32[]{:S(2)}, u32[]{:S(2)}) collective-permute-start(bf16[64,2304]{1,0:T(8,128)(2,1)} %get-tuple-element.57), channel_id=1, source_target_pairs={{0,8},{2,10},{4,12},{6,14},{8,16},{10,18},{12,20},{14,22},{16,24},... | collective-permute-start | bytes 884744 | tf_op jit(solution)/shard_map/ppermute | solution.py:284
  516.2 61.6 %collective-permute-start.89 = (bf16[64,2304]{1,0:T(8,128)(2,1)}, bf16[64,2304]{1,0:T(8,128)(2,1)}, u32[]{:S(2)}, u32[]{:S(2)}) collective-permute-start(bf16[64,2304]{1,0:T(8,128)(2,1)} %get-tuple-element.62), channel_id=1, source_target_pairs={{16,8},{18,10},{20,12},{22,14},{24,16},{26,18},{28,20},{30,22},{17... | collective-permute-start | bytes 884744 | tf_op jit(solution)/shard_map/ppermute | solution.py:284
  600.1 104.8 %collective-permute-start.37 = (bf16[1024,1024]{1,0:T(8,128)(2,1)S(1)}, bf16[1024,1024]{1,0:T(8,128)(2,1)S(1)}, u32[]{:S(2)}, u32[]{:S(2)}) collective-permute-start(bf16[1024,1024]{1,0:T(8,128)(2,1)S(1)} %slice.195), channel_id=1, source_target_pairs={{0,1},{1,0},{2,3},{3,2},{4,5},{5,4},{6,7},{7,6},{8,9},{9,8},{10,11... | collective-permute-start | bytes 6291464 | tf_op jit(solution)/shard_map/ppermute | solution.py:276
  602.3 28.0 %collective-permute-start.97 = (bf16[2,32,2304]{2,1,0:T(8,128)(2,1)S(1)}, bf16[2,32,2304]{2,1,0:T(8,128)(2,1)S(1)}, u32[]{:S(2)}, u32[]{:S(2)}) collective-permute-start(bf16[2,32,2304]{2,1,0:T(8,128)(2,1)S(1)} %dynamic-slice_bitcast_fusion.11), channel_id=1, source_target_pairs={{0,2},{2,0},{4,6},{6,4},{8,10},{10,8},{12,14},{14,12},{16,18},{18,... | collective-permute-start | bytes 884744 | tf_op jit(solution)/shard_map/ppermute | solution.py:280
  603.5 28.6 %collective-permute-start.99 = (bf16[2,32,2304]{2,1,0:T(8,128)(2,1)S(1)}, bf16[2,32,2304]{2,1,0:T(8,128)(2,1)S(1)}, u32[]{:S(2)}, u32[]{:S(2)}) collective-permute-start(bf16[2,32,2304]{2,1,0:T(8,128)(2,1)S(1)} %dynamic-slice_bitcast_fusion.10), channel_id=1, source_target_pairs={{0,4},{2,6},{4,0},{6,2},{8,12},{10,14},{12,8},{14,10},{16,20},{18,... | collective-permute-start | bytes 884744 | tf_op jit(solution)/shard_map/ppermute | solution.py:280
  678.3 29.6 %collective-permute-start.55 = (bf16[64,512]{1,0:T(8,128)(2,1)S(1)}, bf16[64,512]{1,0:T(8,128)(2,1)S(1)}, u32[]{:S(2)}, u32[]{:S(2)}) collective-permute-start(bf16[64,512]{1,0:T(8,128)(2,1)S(1)} %get-tuple-element.89), channel_id=1, source_target_pairs={{0,8},{2,10},{4,12},{6,14},{8,16},{10,18},{12,20},{14,22},{16,24},... | collective-permute-start | bytes 196616 | tf_op jit(solution)/shard_map/ppermute | solution.py:284
  (150 other events, 2696.6 us)

commit v2 on v0

--- a/solution.py
+++ b/solution.py
@@ -1,6 +1,10 @@
+import functools
+
 import jax
 import jax.numpy as jnp
 from jax import lax
+from jax.experimental import pallas as pl
+from jax.experimental.pallas import tpu as pltpu
 from jax.sharding import PartitionSpec as P
 
 LEN = 1024
@@ -272,9 +276,720 @@
     )
 
 
+def exchange(values):
+    return lax.ppermute(values, "tensor", [(0, 1), (1, 0)])
+
+
+def across(values, bit):
+    return lax.ppermute(values, "dp", [(place, place ^ bit) for place in range(16)])
+
+
+def between(values, steps):
+    pairs = [
+        (place, place + 4 * shift)
+        for level, shift in steps
+        for place in range(4 * level, 4 * level + 4)
+    ]
+    return lax.ppermute(values, "dp", pairs)
+
+
+def place_bits():
+    place = lax.axis_index("dp")
+    return place // 4, (place // 2) % 2, place % 2
+
+
+def in_order(own_bit, own, other):
+    return jnp.where(
+        own_bit == 0, jnp.concatenate([own, other], 0), jnp.concatenate([other, own], 0)
+    )
+
+
+def tie(*values):
+    return lax.optimization_barrier(values)
+
+
+def add_wide(first, second):
+    return first.astype(jnp.float32) + second.astype(jnp.float32)
+
+
+def narrow(values):
+    return values.astype(jnp.bfloat16)
+
+
+def gather_direct(values):
+    ups = [between(values, [(z, s) for z in range(4 - s)]) for s in (1, 2, 3)]
+    downs = [between(values, [(z, -s) for z in range(s, 4)]) for s in (1, 2, 3)]
+    line = jnp.stack(ups[::-1] + [values] + downs)
+    return lax.dynamic_slice_in_dim(line, 3 - place_bits()[0], 4, 0)
+
+
+def line_near(values):
+    return in_order(place_bits()[0] % 2, values[None], across(values, 4)[None])
+
+
+def line_middle(near):
+    return between(near, [(1, 1), (2, -1)])
+
+
+def line_far(near, middle):
+    level = place_bits()[0]
+    outer = between(middle, [(1, -1), (2, 1)])
+    far = jnp.where((level == 1) | (level == 2), middle, outer)
+    return in_order(level // 2, near, far)
+
+
+def gather_pair(values, bit):
+    own_bit = place_bits()[2 if bit == 1 else 1]
+    return in_order(own_bit, values[None], across(values, bit)[None])
+
+
+def pick(values, index):
+    return lax.dynamic_index_in_dim(values, index, 0, keepdims=False)
+
+
+def reduce_pair(values, bit):
+    own_bit = place_bits()[2 if bit == 1 else 1]
+    return narrow(add_wide(pick(values, own_bit), across(pick(values, 1 - own_bit), bit)))
+
+
+def reduce_far(values):
+    half = place_bits()[0] // 2
+    mine = lax.dynamic_slice_in_dim(values, 2 * half, 2, 0)
+    theirs = lax.dynamic_slice_in_dim(values, 2 - 2 * half, 2, 0)
+    return mine, narrow(add_wide(theirs, between(theirs, [(0, 1), (3, -1)])))
+
+
+def reduce_middle(mine, theirs):
+    return narrow(add_wide(mine, between(theirs, [(1, 1), (2, -1)])))
+
+
+def reduce_near(mine):
+    bit = place_bits()[0] % 2
+    return add_wide(pick(mine, bit), across(pick(mine, 1 - bit), 4))
+
+
+def reduce_direct(values):
+    level = place_bits()[0]
+    total = pick(values, level).astype(jnp.float32)
+    for s in (1, 2, 3):
+        upper, lower = jnp.minimum(level + s, 3), jnp.maximum(level - s, 0)
+        total = total + between(pick(values, upper), [(z, s) for z in range(4 - s)]).astype(
+            jnp.float32
+        )
+        total = total + between(pick(values, lower), [(z, -s) for z in range(s, 4)]).astype(
+            jnp.float32
+        )
+    return total
+
+
+def sum_all(values):
+    for bit in (1, 2, 4, 8):
+        values = values + across(values, bit)
+    return values
+
+
+TILE = 256
+TOKEN_BLOCK = 512
+ROW_BLOCK = 256
+VMEM_LIMIT = 60 * 1024 * 1024
+
+
+def wide_dot(left, right):
+    return jnp.dot(left, right, preferred_element_type=jnp.float32)
+
+
+def wide_dot_t(left, right):
+    return lax.dot_general(
+        left, right, (((1,), (1,)), ((), ())), preferred_element_type=jnp.float32
+    )
+
+
+def unit_and_inverse(rows):
+    inverse = lax.rsqrt(jnp.mean(rows * rows, axis=-1, keepdims=True) + eps)
+    return rows * inverse, inverse
+
+
+def norm_kernel(tokens, gain, normed):
+    unit, _ = unit_and_inverse(tokens[...].astype(jnp.float32))
+    normed[...] = narrow(unit * gain[...])
+
+
+def middle_kernel(tokens, own, other, gain, middle, normed):
+    rows = tokens[...].astype(jnp.float32) + (own[...] + other[...].astype(jnp.float32))
+    middle[...] = rows
+    unit, _ = unit_and_inverse(rows)
+    normed[...] = narrow(unit * gain[...])
+
+
+def norm_back(rows, grad, gain, gain_grad):
+    unit, inverse = unit_and_inverse(rows)
+
+    @pl.when(pl.program_id(0) == 0)
+    def _():
+        gain_grad[...] = jnp.zeros_like(gain_grad)
+
+    gain_grad[...] += jnp.sum(grad * unit, axis=0, keepdims=True)
+    grad_unit = grad * gain
+    along = jnp.mean(grad_unit * unit, axis=-1, keepdims=True)
+    return inverse * (grad_unit - unit * along)
+
+
+def middle_back_kernel(own, other, middle, gain, out_grad, grad_middle, narrowed, gain_grad):
+    grad = own[...] + other[...].astype(jnp.float32)
+    total = out_grad[...].astype(jnp.float32) + norm_back(
+        middle[...], grad, gain[...], gain_grad
+    )
+    grad_middle[...] = total
+    narrowed[...] = narrow(total)
+
+
+def input_back_kernel(own, other, tokens, gain, grad_middle, input_grad, gain_grad):
+    grad = own[...] + other[...].astype(jnp.float32)
+    input_grad[...] = grad_middle[...] + norm_back(
+        tokens[...].astype(jnp.float32), grad, gain[...], gain_grad
+    )
+
+
+def work(matmul_rows, depth, columns, moved):
+    return pl.CostEstimate(
+        flops=2 * matmul_rows * depth * columns, transcendentals=0, bytes_accessed=moved
+    )
+
+
+def both_kernel(own, other, group, group_t):
+    half = pl.num_programs(0) // 2
+
+    @pl.when(pl.program_id(0) < half)
+    def _():
+        group[...] = own[...]
+        group_t[...] = own[...].T
+
+    @pl.when(pl.program_id(0) >= half)
+    def _():
+        group[...] = other[...]
+        group_t[...] = other[...].T
+
+
+def both_call(own, other):
+    rows, width = own.shape
+    steps = rows // ROW_BLOCK
+    return pl.pallas_call(
+        both_kernel,
+        out_shape=[
+            jax.ShapeDtypeStruct((2 * rows, width), own.dtype),
+            jax.ShapeDtypeStruct((width, 2 * rows), own.dtype),
+        ],
+        grid=(2 * steps,),
+        in_specs=[
+            pl.BlockSpec((ROW_BLOCK, width), lambda i: (jnp.minimum(i, steps - 1), 0)),
+            pl.BlockSpec((ROW_BLOCK, width), lambda i: (jnp.maximum(i - steps, 0), 0)),
+        ],
+        out_specs=[
+            pl.BlockSpec((ROW_BLOCK, width), lambda i: (i, 0)),
+            pl.BlockSpec((width, ROW_BLOCK), lambda i: (0, i)),
+        ],
+        compiler_params=pltpu.CompilerParams(vmem_limit_bytes=VMEM_LIMIT),
+        cost_estimate=work(0, 0, 0, 12 * rows * width),
+        name="both",
+    )(own, other)
+
+
+def row_call(kernel, name, args, outs):
+    tokens = args[0].shape[0]
+    spec = lambda shape: (
+        pl.BlockSpec((ROW_BLOCK, shape[1]), lambda i: (i, 0))
+        if shape[0] == tokens
+        else pl.BlockSpec(shape, lambda i: (0, 0))
+    )
+    return pl.pallas_call(
+        kernel,
+        out_shape=[jax.ShapeDtypeStruct(*out) for out in outs],
+        grid=(tokens // ROW_BLOCK,),
+        in_specs=[spec(arg.shape) for arg in args],
+        out_specs=[spec(out[0]) for out in outs],
+        compiler_params=pltpu.CompilerParams(vmem_limit_bytes=VMEM_LIMIT),
+        cost_estimate=work(0, 0, 0, 16 * tokens * args[0].shape[1]),
+        name=name,
+    )(*args)
+
+
+def place_pieces(weights, kinds, bits, first, second, first_kinds):
+    x_bit, y_bit = bits[0], bits[1]
+    for side in range(2):
+        for z in range(4):
+            for kind in range(kinds):
+                if kind < first_kinds:
+                    weights[kind, z, side, pl.ds(x_bit, 1)] = first[0][side, z, kind][None]
+                    weights[kind, z, side, pl.ds(1 - x_bit, 1)] = first[1][side, z, kind][None]
+                else:
+                    at = kind - first_kinds
+                    weights[kind, z, pl.ds(y_bit, 1), side] = second[0][side, z, at][None]
+                    weights[kind, z, pl.ds(1 - y_bit, 1), side] = second[1][side, z, at][None]
+
+
+def cut_first(product, kind, bits, send, keep, at):
+    for side in range(2):
+        for z in range(4):
+            keep[side, z, at] = product[kind, z, side, pl.ds(bits[0], 1)][0]
+            send[side, z, at] = product[kind, z, side, pl.ds(1 - bits[0], 1)][0]
+
+
+def cut_second(product, kind, bits, send, keep, at):
+    for side in range(2):
+        for z in range(4):
+            keep[side, z, at] = product[kind, z, pl.ds(bits[1], 1), side][0]
+            send[side, z, at] = product[kind, z, pl.ds(1 - bits[1], 1), side][0]
+
+
+def ffn_kernel(bits, normed, cotangent, normed_t, cotangent_t, shards, *rest, pairs, carried):
+    if carried:
+        carry_in, rest = rest[:2], rest[2:]
+    outs, rest = rest[: 4 if pairs else 1], rest[4 if pairs else 1 :]
+    totals_out, scratch = rest[: 4 if pairs else 2], rest[4 if pairs else 2 :]
+    weights, made, totals, product, narrowed, sems = scratch
+    step, last = pl.program_id(0), pl.num_programs(0) - 1
+    tokens, width = normed.shape
+    shard = shards.shape[2]
+    own = tokens // 2
+    loads = []
+    if carried:
+        loads = [pltpu.make_async_copy(carry_in[i], totals.at[i], sems.at[i]) for i in range(2)]
+    if pairs:
+        saves = [
+            pltpu.make_async_copy(totals.at[i, pl.ds(0, own)], totals_out[i], sems.at[i])
+            for i in range(2)
+        ] + [
+            pltpu.make_async_copy(narrowed.at[i], totals_out[2 + i], sems.at[2 + i])
+            for i in range(2)
+        ]
+    else:
+        saves = [pltpu.make_async_copy(totals.at[i], totals_out[i], sems.at[i]) for i in range(2)]
+
+    @pl.when(step == 0)
+    def _():
+        for copy in loads:
+            copy.start()
+        if not carried:
+            totals[...] = jnp.zeros_like(totals)
+
+    for place in range(shards.shape[0]):
+        for kind in range(3):
+            weights[kind, place * shard : (place + 1) * shard] = shards[place, kind]
+
+    for block in range(tokens // TOKEN_BLOCK):
+        at = slice(block * TOKEN_BLOCK, (block + 1) * TOKEN_BLOCK)
+        gate = wide_dot(normed[at], weights[0])
+        up = wide_dot(normed[at], weights[1])
+        grad = wide_dot(cotangent[at], weights[2])
+        sigm = 0.5 + 0.5 * jnp.tanh(0.5 * gate)
+        silu = gate * sigm
+        made[0, at] = narrow(grad * up * (sigm + silu * (1.0 - sigm)))
+        made[1, at] = narrow(grad * silu)
+        made[2, at] = narrow(silu * up)
+
+    @pl.when(step == 0)
+    def _():
+        for copy in loads:
+            copy.wait()
+
+    for block in range(tokens // TOKEN_BLOCK):
+        at = slice(block * TOKEN_BLOCK, (block + 1) * TOKEN_BLOCK)
+        totals[0, at] += wide_dot_t(made[2, at], weights[2])
+        totals[1, at] += wide_dot_t(made[0, at], weights[0]) + wide_dot_t(
+            made[1, at], weights[1]
+        )
+
+    @pl.when(step == last)
+    def _():
+        if pairs:
+            narrowed[...] = narrow(totals[:, own:])
+        for copy in saves:
+            copy.start()
+
+    for kind in range(3):
+        left = cotangent_t if kind == 2 else normed_t
+        made_grad = narrow(wide_dot(left[...], made[kind]))
+        if pairs:
+            product[kind] = made_grad.reshape(product.shape[1:])
+        else:
+            for place in range(shards.shape[0]):
+                outs[0][place, kind] = made_grad[place * shard : (place + 1) * shard]
+
+    if pairs:
+        first_tiles = pairs
+
+        @pl.when(step < first_tiles)
+        def _():
+            for kind in range(3):
+                cut_first(product, kind, bits, outs[0], outs[1], kind)
+
+        @pl.when(step >= first_tiles)
+        def _():
+            for kind in range(3):
+                cut_second(product, kind, bits, outs[2], outs[3], kind)
+
+    @pl.when(step == last)
+    def _():
+        for copy in saves:
+            copy.wait()
+
+
+def ffn_call(bits, rows, rows_t, shards, pairs=False, carry=()):
+    tokens, width = rows[0].shape
+    places, _, shard, units = shards.shape
+    tiles = units // TILE
+    whole = pl.BlockSpec((tokens, width), lambda i, b: (0, 0), pipeline_mode=pl.Buffered(1))
+    whole_t = pl.BlockSpec((width, tokens), lambda i, b: (0, 0), pipeline_mode=pl.Buffered(1))
+    natural = pl.BlockSpec((places, 3, shard, TILE), lambda i, b: (0, 0, 0, i))
+    anywhere = pl.BlockSpec(memory_space=pl.ANY)
+    own = tokens // 2
+    shape = lambda *dims, dtype=jnp.bfloat16: jax.ShapeDtypeStruct(dims, dtype)
+    if pairs:
+        first_tiles = tiles // 2
+        piece = (2, 4, 3, shard)
+        first_spec = pl.BlockSpec(
+            piece + (TILE,), lambda i, b: (0, 0, 0, 0, jnp.minimum(i, first_tiles - 1))
+        )
+        second_spec = pl.BlockSpec(
+            piece + (TILE,), lambda i, b: (0, 0, 0, 0, jnp.maximum(i - first_tiles, 0))
+        )
+        out_specs = [first_spec] * 2 + [second_spec] * 2 + [anywhere] * 4
+        first_shape = shape(*piece, first_tiles * TILE)
+        second_shape = shape(*piece, units - first_tiles * TILE)
+        out_shape = [first_shape] * 2 + [second_shape] * 2
+        out_shape += [shape(own, width, dtype=jnp.float32)] * 2 + [shape(own, width)] * 2
+    else:
+        first_tiles = 0
+        out_specs = [natural] + [anywhere] * 2
+        out_shape = [shape(*shards.shape)] + [shape(tokens, width, dtype=jnp.float32)] * 2
+    return pl.pallas_call(
+        functools.partial(ffn_kernel, pairs=first_tiles, carried=bool(carry)),
+        out_shape=out_shape,
+        grid_spec=pltpu.PrefetchScalarGridSpec(
+            num_scalar_prefetch=1,
+            grid=(tiles,),
+            in_specs=[whole] * 2 + [whole_t] * 2 + [natural] + [anywhere] * len(carry),
+            out_specs=out_specs,
+            scratch_shapes=[
+                pltpu.VMEM((3, width, TILE), jnp.bfloat16),
+                pltpu.VMEM((3, tokens, TILE), jnp.bfloat16),
+                pltpu.VMEM((2, tokens, width), jnp.float32),
+                pltpu.VMEM((3, 4, 2, 2, shard, TILE), jnp.bfloat16),
+                pltpu.VMEM((2, own, width) if pairs else (2, 16, 128), jnp.bfloat16),
+                pltpu.SemaphoreType.DMA((4,)),
+            ],
+        ),
+        compiler_params=pltpu.CompilerParams(
+            dimension_semantics=("arbitrary",), vmem_limit_bytes=VMEM_LIMIT
+        ),
+        cost_estimate=work(tokens, width, 9 * units, 40 * tokens * width),
+        name="ffn",
+    )(bits, *rows, *rows_t, shards, *carry)
+
+
+def earlier(values, steps):
+    row = lax.broadcasted_iota(jnp.int32, values.shape, 0)
+    return jnp.where(row >= steps, pltpu.roll(values, steps, 0), 0.0)
+
+
+def later(values, steps):
+    rows = values.shape[0]
+    row = lax.broadcasted_iota(jnp.int32, values.shape, 0)
+    return jnp.where(row < rows - steps, pltpu.roll(values, rows - steps, 0), 0.0)
+
+
+def convolve(mixed, taps):
+    return taps[0:1] * earlier(mixed, 2) + taps[1:2] * earlier(mixed, 1) + taps[2:3] * mixed
+
+
+def mixer_kernel(
+    bits, normed, taps, first_own, first_other, second_own, second_other,
+    saved, kept_weights, own_out, other_out, weights, total,
+):
+    step, last = pl.program_id(0), pl.num_programs(0) - 1
+    place_pieces(weights, 4, bits, (first_own, first_other), (second_own, second_other), 2)
+    width = normed.shape[1]
+    for kind in range(4):
+        kept_weights[kind] = weights[kind].reshape(width, TILE)
+
+    @pl.when(step == 0)
+    def _():
+        total[...] = jnp.zeros_like(total)
+
+    tap_rows = taps[...].astype(jnp.float32)
+    for block in range(normed.shape[0] // LEN):
+        at = slice(block * LEN, (block + 1) * LEN)
+        b_rows = wide_dot(normed[at], kept_weights[0])
+        x_rows = wide_dot(normed[at], kept_weights[2])
+        c_rows = wide_dot(normed[at], kept_weights[1])
+        saved[0, at], saved[1, at], saved[2, at] = b_rows, c_rows, x_rows
+        gated = narrow(c_rows * convolve(b_rows * x_rows, tap_rows))
+        total[at] += wide_dot_t(gated, kept_weights[3])
+
+    @pl.when(step == last)
+    def _():
+        own = total.shape[0] // 2
+        own_out[...] = total[:own]
+        other_out[...] = narrow(total[own:])
+
+
+def mixer_call(bits, normed, taps, first, second):
+    tokens, width = normed.shape
+    shard, channels = first[0].shape[3:]
+    own = tokens // 2
+    still = lambda *dims: pl.BlockSpec(dims, lambda i, b: (0,) * len(dims), pipeline_mode=pl.Buffered(1))
+    piece = pl.BlockSpec((2, 4, 2, shard, TILE), lambda i, b: (0, 0, 0, 0, i))
+    return pl.pallas_call(
+        mixer_kernel,
+        out_shape=[
+            jax.ShapeDtypeStruct((3, tokens, channels), jnp.float32),
+            jax.ShapeDtypeStruct((4, width, channels), jnp.bfloat16),
+            jax.ShapeDtypeStruct((own, width), jnp.float32),
+            jax.ShapeDtypeStruct((own, width), jnp.bfloat16),
+        ],
+        grid_spec=pltpu.PrefetchScalarGridSpec(
+            num_scalar_prefetch=1,
+            grid=(channels // TILE,),
+            in_specs=[still(tokens, width), pl.BlockSpec((3, TILE), lambda i, b: (0, i))]
+            + [piece] * 4,
+            out_specs=[
+                pl.BlockSpec((3, tokens, TILE), lambda i, b: (0, 0, i)),
+                pl.BlockSpec((4, width, TILE), lambda i, b: (0, 0, i)),
+                pl.BlockSpec((own, width), lambda i, b: (0, 0)),
+                pl.BlockSpec((own, width), lambda i, b: (0, 0)),
+            ],
+            scratch_shapes=[
+                pltpu.VMEM((4, 4, 2, 2, shard, TILE), jnp.bfloat16),
+                pltpu.VMEM((tokens, width), jnp.float32),
+            ],
+        ),
+        compiler_params=pltpu.CompilerParams(
+            dimension_semantics=("arbitrary",), vmem_limit_bytes=VMEM_LIMIT
+        ),
+        cost_estimate=work(tokens, width, 4 * channels, 40 * tokens * width),
+        name="mixer",
+    )(bits, normed, taps, *first, *second)
+
+
+def mixer_back_kernel(
+    bits, grads, grads_t, normed_t, taps, saved, weights,
+    first_send, first_keep, second_send, second_keep, own_out, other_out, taps_grad,
+    made, product, total,
+):
+    step, last = pl.program_id(0), pl.num_programs(0) - 1
+
+    @pl.when(step == 0)
+    def _():
+        total[...] = jnp.zeros_like(total)
+
+    tap_rows = taps[...].astype(jnp.float32)
+    tap_sums = [jnp.zeros((1, TILE), jnp.float32) for _ in range(3)]
+    for block in range(grads.shape[0] // LEN):
+        at = slice(block * LEN, (block + 1) * LEN)
+        grad_gated = wide_dot(grads[at], weights[3])
+        b_rows, c_rows, x_rows = saved[0, at], saved[1, at], saved[2, at]
+        mixed = b_rows * x_rows
+        shifted = [earlier(mixed, 2), earlier(mixed, 1), mixed]
+        convolved = sum(tap_rows[k : k + 1] * shifted[k] for k in range(3))
+        grad_conv = grad_gated * c_rows
+        tap_sums = [
+            tap_sums[k] + jnp.sum(grad_conv * shifted[k], axis=0, keepdims=True) for k in range(3)
+        ]
+        grad_mixed = (
+            tap_rows[0:1] * later(grad_conv, 2)
+            + tap_rows[1:2] * later(grad_conv, 1)
+            + tap_rows[2:3] * grad_conv
+        )
+        made[0, at] = narrow(grad_mixed * x_rows)
+        made[1, at] = narrow(grad_gated * convolved)
+        made[2, at] = narrow(grad_mixed * b_rows)
+        made[3, at] = narrow(c_rows * convolved)
+    for k in range(3):
+        taps_grad[k : k + 1] = tap_sums[k]
+    for block in range(grads.shape[0] // TOKEN_BLOCK):
+        at = slice(block * TOKEN_BLOCK, (block + 1) * TOKEN_BLOCK)
+        total[at] += (
+            wide_dot_t(made[0, at], weights[0])
+            + wide_dot_t(made[1, at], weights[1])
+            + wide_dot_t(made[2, at], weights[2])
+        )
+
+    @pl.when(step == last)
+    def _():
+        own = total.shape[0] // 2
+        own_out[...] = total[:own]
+        other_out[...] = narrow(total[own:])
+
+    for kind in range(4):
+        left = grads_t if kind == 3 else normed_t
+        product[kind] = narrow(wide_dot(left[...], made[kind])).reshape(product.shape[1:])
+        if kind < 2:
+            cut_first(product, kind, bits, first_send, first_keep, kind)
+        else:
+            cut_second(product, kind, bits, second_send, second_keep, kind - 2)
+
+
+def mixer_back_call(bits, grads, grads_t, normed_t, taps, saved, weights):
+    tokens, width = grads.shape
+    channels = taps.shape[1]
+    shard = width // 16
+    own = tokens // 2
+    still = lambda *dims: pl.BlockSpec(dims, lambda i, b: (0,) * len(dims), pipeline_mode=pl.Buffered(1))
+    piece = pl.BlockSpec((2, 4, 2, shard, TILE), lambda i, b: (0, 0, 0, 0, i))
+    return pl.pallas_call(
+        mixer_back_kernel,
+        out_shape=[jax.ShapeDtypeStruct((2, 4, 2, shard, channels), jnp.bfloat16)] * 4
+        + [
+            jax.ShapeDtypeStruct((own, width), jnp.float32),
+            jax.ShapeDtypeStruct((own, width), jnp.bfloat16),
+            jax.ShapeDtypeStruct((3, channels), jnp.float32),
+        ],
+        grid_spec=pltpu.PrefetchScalarGridSpec(
+            num_scalar_prefetch=1,
+            grid=(channels // TILE,),
+            in_specs=[
+                still(tokens, width),
+                still(width, tokens),
+                still(width, tokens),
+                pl.BlockSpec((3, TILE), lambda i, b: (0, i)),
+                pl.BlockSpec((3, tokens, TILE), lambda i, b: (0, 0, i)),
+                pl.BlockSpec((4, width, TILE), lambda i, b: (0, 0, i)),
+            ],
+            out_specs=[piece] * 4
+            + [
+                pl.BlockSpec((own, width), lambda i, b: (0, 0)),
+                pl.BlockSpec((own, width), lambda i, b: (0, 0)),
+                pl.BlockSpec((3, TILE), lambda i, b: (0, i)),
+            ],
+            scratch_shapes=[
+                pltpu.VMEM((4, tokens, TILE), jnp.bfloat16),
+                pltpu.VMEM((4, 4, 2, 2, shard, TILE), jnp.bfloat16),
+                pltpu.VMEM((tokens, width), jnp.float32),
+            ],
+        ),
+        compiler_params=pltpu.CompilerParams(
+            dimension_semantics=("arbitrary",), vmem_limit_bytes=VMEM_LIMIT
+        ),
+        cost_estimate=work(tokens, width, 9 * channels, 40 * tokens * width),
+        name="mixer_back",
+    )(bits, grads, grads_t, normed_t, taps, saved, weights)
+
+
+def per_device_pairs(
+    tokens,
+    norm_gain1,
+    in_weight,
+    conv_kernel,
+    out_weight,
+    norm_gain2,
+    gate_up_weight,
+    down_weight,
+    out_grad,
+):
+    rows, width = tokens.shape
+    split = down_weight.shape[1] // (2 * TILE) * TILE
+    collect = lambda values: both_call(values, exchange(values))
+    bits = jnp.stack(place_bits()[:0:-1]).astype(jnp.int32)
+    gain1, gain2 = norm_gain1[None], norm_gain2[None]
+    wide_rows = ((rows, width), jnp.float32)
+    narrow_rows = ((rows, width), jnp.bfloat16)
+    gain_row = ((1, width), jnp.float32)
+
+    small = jnp.concatenate([jnp.transpose(in_weight, (1, 0, 2)), out_weight[None]], 0)
+    big = jnp.concatenate([jnp.transpose(gate_up_weight, (1, 0, 2)), down_weight[None]], 0)
+    big1 = lax.all_gather(big[..., :split], "dp", axis=0)
+    big2 = lax.all_gather(big[..., split:], "dp", axis=0)
+
+    near = line_near(small)
+    (normed1,) = row_call(norm_kernel, "norm", (tokens, gain1), (narrow_rows,))
+    group_n1, normed1_t = collect(normed1)
+    lines = line_far(near, line_middle(near))
+    lines, group_n1 = tie(lines, group_n1)
+    s_first, s_second = gather_pair(lines[:, :2], 2), gather_pair(lines[:, 2:], 1)
+    group_grad, cotangent_t = collect(out_grad)
+    s_first, s_second, group_grad, cotangent_t, normed1_t = tie(
+        s_first, s_second, group_grad, cotangent_t, normed1_t
+    )
+    s_first, s_second = (s_first, across(s_first, 1)), (s_second, across(s_second, 2))
+    saved, mixer_weights, own, other = mixer_call(bits, group_n1, conv_kernel, s_first, s_second)
+    middle, normed2 = row_call(
+        middle_kernel, "middle", (tokens, own, exchange(other), gain2), (wide_rows, narrow_rows)
+    )
+    group_n2, normed2_t = collect(normed2)
+    rows_both, rows_t = (group_n2, group_grad), (normed2_t, cotangent_t)
+
+    grads1, *carry = ffn_call(bits, rows_both, rows_t, big1)
+    grads1 = lax.psum_scatter(grads1, "dp", scatter_dimension=0)
+    send2, keep2, send2b, keep2b, forward, backward, forward_other, backward_other = ffn_call(
+        bits, rows_both, rows_t, big2, True, tuple(carry)
+    )
+    backward_other = exchange(backward_other)
+    took2, took2b = across(send2, 1), across(send2b, 2)
+    grad_middle, narrowed, gain_two_grad = row_call(
+        middle_back_kernel,
+        "middle_back",
+        (backward, backward_other, middle, gain2, out_grad),
+        (wide_rows, narrow_rows, gain_row),
+    )
+    group_gm, grads_t = collect(narrowed)
+    s_send, s_keep, s_sendb, s_keepb, own, other, kernel_grad = mixer_back_call(
+        bits, group_gm, grads_t, normed1_t, conv_kernel, saved, mixer_weights
+    )
+    took2, took2b, s_send, s_keep, s_sendb, s_keepb, own, other, kernel_grad = tie(
+        took2, took2b, s_send, s_keep, s_sendb, s_keepb, own, other, kernel_grad
+    )
+
+    first2, second2 = narrow(add_wide(keep2, took2)), narrow(add_wide(keep2b, took2b))
+    first2, second2 = reduce_pair(first2, 2), reduce_pair(second2, 1)
+    s_first = narrow(add_wide(s_keep, across(s_send, 1)))
+    s_second = narrow(add_wide(s_keepb, across(s_sendb, 2)))
+    input_grad, gain_one_grad = row_call(
+        input_back_kernel,
+        "input_back",
+        (own, exchange(other), tokens, gain1, grad_middle),
+        (wide_rows, gain_row),
+    )
+    summed = jnp.concatenate([gain_one_grad, gain_two_grad, kernel_grad.reshape(1, -1)], 1)
+    first2, second2, s_first, s_second, summed = tie(first2, second2, s_first, s_second, summed)
+
+    s_first, s_second = reduce_pair(s_first, 2), reduce_pair(s_second, 1)
+    mine2, theirs2 = reduce_far(jnp.concatenate([first2, second2], -1))
+    result = narrow(middle + (forward + exchange(forward_other).astype(jnp.float32)))
+    summed = summed + across(summed, 1)
+    summed = summed + across(summed, 2)
+    s_first, s_second, mine2, theirs2, summed, result = tie(
+        s_first, s_second, mine2, theirs2, summed, result
+    )
+
+    mine_s, theirs_s = reduce_far(jnp.concatenate([s_first, s_second], 1))
+    mine2 = reduce_middle(mine2, theirs2)
+    summed = summed + across(summed, 4)
+    mine_s, theirs_s, mine2, summed = tie(mine_s, theirs_s, mine2, summed)
+    grads2 = reduce_near(mine2)
+    mine_s = reduce_middle(mine_s, theirs_s)
+    summed = summed + across(summed, 8)
+    mine_s, grads2, summed = tie(mine_s, grads2, summed)
+    small_grads = reduce_near(mine_s)
+    gains = summed[0, : 2 * width]
+    gains = gains + exchange(gains)
+    big_grads = jnp.concatenate([grads1.astype(jnp.float32), grads2], -1)
+    return (
+        result,
+        input_grad,
+        gains[:width],
+        jnp.transpose(small_grads[:3], (1, 0, 2)),
+        summed[0, 2 * width :].reshape(kernel_grad.shape),
+        small_grads[3],
+        gains[width:],
+        jnp.transpose(big_grads[:2], (1, 0, 2)),
+        big_grads[2],
+    )
+
+
 def solution(mesh):
+    paired = mesh.shape["dp"] == 16 and mesh.shape["tensor"] == 2
     return jax.shard_map(
-        per_device,
+        per_device_pairs if paired else per_device,
         mesh=mesh,
         in_specs=(
             P(("dp", "tensor"), None),

time: 1320 us -> 566 us (0.43)
  waiting for transfers between devices: 950 us -> 216 us
  Pallas kernels: 0 us -> 237 us
  matrix products: 215 us -> 0 us
  starting transfers between devices: 1.03 us -> 46 us
  blocking collectives: 44.9 us -> 0 us
  other arithmetic: 55.8 us -> 30.7 us
  local copies, waits for them, and re-layouts: 28.4 us -> 13.1 us
    reduce_scatter x7 -> x1, waiting for transfers between devices: 430 us -> 0.01 us  [per_device_pairs(): grads1 = lax.psum_scatter(grads1, 'dp', scatter_dimension=0)]
    all_gather x8 -> x2, waiting for transfers between devices: 344 us -> 0.02 us  [the longest x1 0.02 us: per_device_pairs(): big2 = lax.all_gather(big[..., split:], 'dp', axis=0)]
    pallas_call x0 -> x12, Pallas kernels: none -> 237 us  [the longest x2 119 us: ffn_call(): pl.pallas_call(functools.partial(ffn_kernel, pairs=first_tiles, carried=b...]
    ppermute x0 -> x34, waiting for transfers between devices: none -> 216 us  [the longest x19 144 us: across(): lax.ppermute(values, 'dp', [(place, place ^ bit) for place in range(16)])]
    dot_general x12 -> x0, matrix products: 215 us -> none  [the longest x1 37.6 us: ffn_back_term(): jnp.einsum('tkf,dkf->td', grad_gate_up, gate_up_w, preferred_element_type...]
    unnamed x17 -> x3, waiting for transfers between devices: 176 us -> 0.05 us
    ppermute x0 -> x34, starting transfers between devices: none -> 45.9 us  [the longest x19 28.5 us: across(): lax.ppermute(values, 'dp', [(place, place ^ bit) for place in range(16)])]
    psum x1 -> x0, blocking collectives: 44.9 us -> none  [per_device(): lax.psum((gain_grads[0], gain_grads[1], kernel_full), ('dp', 'tensor'))]
  transfers between devices with their start and end apart: 16 -> 37, of which waited for: 13 -> 18; matrix products, arithmetic and copies ran while one was open for 12% -> 6% of each run, Pallas kernels for 0% -> 29%
where the time goes in v2:
time: 566 us; the launch traced here: 557 us
  Pallas kernels  237 us (42%)
  waiting for transfers between devices  216 us (38%)
  starting transfers between devices  46 us (8%)
  other arithmetic  30.7 us (5%)
  between operations  14.8 us (3%)
  local copies, waits for them, and re-layouts  13.1 us (2%)
    ppermute x19, waiting for transfers between devices, across(): lax.ppermute(values, 'dp', [(place, place ^ bit) for place in range(16)])  144 us
    pallas_call x2, Pallas kernels, ffn_call(): pl.pallas_call(functools.partial(ffn_kernel, pairs=first_tiles, carried=b...  119 us
    ppermute x6, waiting for transfers between devices, between(): return lax.ppermute(values, 'dp', pairs)  57.5 us
    pallas_call x1, Pallas kernels, mixer_back_call(): pl.pallas_call(mixer_back_kernel, out_shape=[jax.ShapeDtypeStruct((2, 4,...  35.1 us
    pallas_call x4, Pallas kernels, both_call(): pl.pallas_call(both_kernel, out_shape=[jax.ShapeDtypeStruct((2 * rows, wi...  32.4 us
    ppermute x19, starting transfers between devices, across(): lax.ppermute(values, 'dp', [(place, place ^ bit) for place in range(16)])  28.5 us
    pallas_call x4, Pallas kernels, row_call(): pl.pallas_call(kernel, out_shape=[jax.ShapeDtypeStruct(*out) for out in o...  27.7 us
    convert_element_type x13, other arithmetic, narrow(): return values.astype(jnp.bfloat16)  22.7 us
  transfers between devices with their start and end apart: 37, of which 18 were waited for; matrix products, arithmetic and copies ran while one was open for 6% of the time, Pallas kernels for 29%

profile of v2, /device:TPU:0, one launch (start us, length us, event | category | flops | bytes accessed | tf_op | source)
XLA Modules:
  0.0 557.3 jit_solution(15156831348456293744)
XLA Ops:
  11.2 4.3 norm.1.own
  18.6 7.9 %collective-permute-done = bf16[4,64,512]{2,1,0:T(8,128)(2,1)S(1)} collective-permute-done((bf16[4,64,512]{2,1,0:T(8,128)(2,1)S(1)}, bf16[4,64,512]{2,1,0:T(8,128)(2,1)S(1)}, u32[]{:S(2)}, u32[]{:S(2)}) %collective-permute-start) | collective-permute-done | bytes 262176 | tf_op jit(solution)/shard_map/ppermute | solution.py:284
  28.7 46.0 %collective-permute-done.2 = bf16[2,4,64,512]{3,2,1,0:T(8,128)(2,1)S(1)} collective-permute-done((bf16[2,4,64,512]{3,2,1,0:T(8,128)(2,1)S(1)}, bf16[2,4,64,512]{3,2,1,0:T(8,128)(2,1)S(1)}, u32[]{:S(2)}, u32[]{:S(2)}) %collective-permute-start.2) | collective-permute-done | bytes 524320 | tf_op jit(solution)/shard_map/ppermute | solution.py:293
  76.1 8.0 %both.4 = (bf16[2048,1024]{1,0:T(8,128)(2,1)}, bf16[1024,2048]{1,0:T(8,128)(2,1)}) custom-call(bf16[1024,1024]{1,0:T(8,128)(2,1)} %norm.1.own, bf16[1024,1024]{1,0:T(8,128)(2,1)} %collective-permute-done.3.other), custom_call_target="tpu_custom_call" | custom-call | bytes 12582912 | tf_op jit(solution)/shard_map/both/pallas_call | solution.py:476
  88.6 8.1 %both.5 = (bf16[2048,1024]{1,0:T(8,128)(2,1)}, bf16[1024,2048]{1,0:T(8,128)(2,1)}) custom-call(bf16[1024,1024]{1,0:T(8,128)(2,1)} %out_grad.1, bf16[1024,1024]{1,0:T(8,128)(2,1)} %collective-permute-done.6.other), custom_call_target="tpu_custom_call" | custom-call | bytes 12582912 | tf_op jit(solution)/shard_map/both/pallas_call | solution.py:476
  96.7 13.0 %collective-permute-done.5 = bf16[4,2,64,512]{3,2,1,0:T(8,128)(2,1)S(1)} collective-permute-done((bf16[4,2,64,512]{3,2,1,0:T(8,128)(2,1)}, bf16[4,2,64,512]{3,2,1,0:T(8,128)(2,1)S(1)}, u32[]{:S(2)}, u32[]{:S(2)}) %collective-permute-start.5) | collective-permute-done | bytes 524320 | tf_op jit(solution)/shard_map/ppermute | solution.py:284
  112.7 22.2 %collective-permute-done.7.first_other = bf16[2,4,2,64,512]{4,3,2,1,0:T(8,128)(2,1)S(1)} collective-permute-done((bf16[2,4,2,64,512]{4,3,2,1,0:T(8,128)(2,1)S(1)}, bf16[2,4,2,64,512]{4,3,2,1,0:T(8,128)(2,1)S(1)}, u32[]{:S(2)}, u32[]{:S(2)}) %collective-permute-start.7) | collective-permute-done | bytes 1048608 | tf_op jit(solution)/shard_map/ppermute | solution.py:284
  136.0 22.2 %mixer.1 = (f32[3,2048,512]{2,1,0:T(8,128)}, bf16[4,1024,512]{2,1,0:T(8,128)(2,1)}, f32[1024,1024]{1,0:T(8,128)}, bf16[1024,1024]{1,0:T(8,128)(2,1)}) custom-call(s32[2]{0:T(128)} %pad_add_fusion.bits, bf16[2048,1024]{1,0:T(8,128)(2,1)} %get-tuple-element.81.normed, bf16[3,512]{1,0:T(4,128)(2,1)} %taps.3, bf16[2,4,2,64,512]{4,3,2,1,0:T(8,128)(2,1)} %copy-done.19, ...), custom_call_target="tpu_custom_call" | custom-call | flops 8589934592 | bytes 83886080 | tf_op jit(solution)/shard_map/mixer/pallas_call | solution.py:742
  158.3 4.4 collective-permute-done.9.other
  163.9 6.6 %middle.1 = (f32[1024,1024]{1,0:T(8,128)}, bf16[1024,1024]{1,0:T(8,128)(2,1)}) custom-call(bf16[1024,1024]{1,0:T(8,128)(2,1)} %tokens.5, f32[1024,1024]{1,0:T(8,128)} %get-tuple-element.88.own, bf16[1024,1024]{1,0:T(8,128)(2,1)} %copy-done.14, f32[1,1024]{1,0:T(1,128)} %bitcast.78), custom_call_target="tpu_custom_call" | custom-call | bytes 16777216 | tf_op jit(solution)/shard_map/middle/pallas_call | solution.py:504
  170.7 4.2 collective-permute-done.10.other
  176.2 8.0 %both.6 = (bf16[2048,1024]{1,0:T(8,128)(2,1)}, bf16[1024,2048]{1,0:T(8,128)(2,1)}) custom-call(bf16[1024,1024]{1,0:T(8,128)(2,1)} %get-tuple-element.90.own, bf16[1024,1024]{1,0:T(8,128)(2,1)} %copy-done.10), custom_call_target="tpu_custom_call" | custom-call | bytes 12582912 | tf_op jit(solution)/shard_map/both/pallas_call | solution.py:476
  184.2 53.7 %ffn.2 = (bf16[16,3,64,1024]{3,2,1,0:T(8,128)(2,1)}, f32[2048,1024]{1,0:T(8,128)}, f32[2048,1024]{1,0:T(8,128)}) custom-call(s32[2]{0:T(128)} %pad_add_fusion.bits, bf16[2048,1024]{1,0:T(8,128)(2,1)} %get-tuple-element.91.normed, bf16[2048,1024]{1,0:T(8,128)(2,1)} %get-tuple-element.92.cotangent, bf16[1024,2048]{1,0:T(8,128)(2,1)} %get-tuple-element.93.normed_t, ...), custom_call_target="tpu_custom_call" | custom-call | flops 38654705664 | bytes 83886080 | tf_op jit(solution)/shard_map/ffn/pallas_call | solution.py:665
  237.9 65.4 %ffn.3 = (bf16[2,4,3,64,512]{4,3,2,1,0:T(8,128)(2,1)}, bf16[2,4,3,64,512]{4,3,2,1,0:T(8,128)(2,1)}, bf16[2,4,3,64,768]{4,3,2,1,0:T(8,128)(2,1)}, bf16[2,4,3,64,7...) custom-call(s32[2]{0:T(128)} %pad_add_fusion.bits, ...), custom_call_target="tpu_custom_call" | custom-call | flops 48318382080 | bytes 83886080 | tf_op jit(solution)/shard_map/ffn/pallas_call | solution.py:665
  303.7 4.1 collective-permute-done.13.other
  309.1 8.7 %middle_back.1 = (f32[1024,1024]{1,0:T(8,128)}, bf16[1024,1024]{1,0:T(8,128)(2,1)}, f32[1,1024]{1,0:T(1,128)}) custom-call(f32[1024,1024]{1,0:T(8,128)} %get-tuple-element.100.own, bf16[1024,1024]{1,0:T(8,128)(2,1)} %copy-done.13, f32[1024,1024]{1,0:T(8,128)} %get-tuple-element.102.middle, f32[1,1024]{1,0:T(1,128)} %bitcast.79, bf16[1024,1024]{1,0:T(8,128)(2,1)} %out_grad.1), custom_call_target="tpu_custom_call" | custom-call | bytes 16777216 | tf_op jit(solution)/shard_map/middle_back/pallas_call | solution.py:504
  322.3 8.4 %both.7 = (bf16[2048,1024]{1,0:T(8,128)(2,1)}, bf16[1024,2048]{1,0:T(8,128)(2,1)}) custom-call(bf16[1024,1024]{1,0:T(8,128)(2,1)} %get-tuple-element.103.own, bf16[1024,1024]{1,0:T(8,128)(2,1)} %collective-permute-done.14.other), custom_call_target="tpu_custom_call" | custom-call | bytes 12582912 | tf_op jit(solution)/shard_map/both/pallas_call | solution.py:476
  330.6 35.1 %mixer_back.1 = (bf16[2,4,2,64,512]{4,3,2,1,0:T(8,128)(2,1)}, bf16[2,4,2,64,512]{4,3,2,1,0:T(8,128)(2,1)}, bf16[2,4,2,64,512]{4,3,2,1,0:T(8,128)(2,1)}, bf16[2,4...) custom-call(s32[2]{0:T(128)} %pad_add_fusion.bits, ...), custom_call_target="tpu_custom_call" | custom-call | flops 19327352832 | bytes 83886080 | tf_op jit(solution)/shard_map/mixer_back/pallas_call | solution.py:839
  365.8 20.0 %collective-permute-done.12 = bf16[2,4,3,64,768]{4,3,2,1,0:T(8,128)(2,1)S(1)} collective-permute-done((bf16[2,4,3,64,768]{4,3,2,1,0:T(8,128)(2,1)}, bf16[2,4,3,64,768]{4,3,2,1,0:T(8,128)(2,1)S(1)}, u32[]{:S(2)}, u32[]{:S(2)}) %collective-permute-start.12) | collective-permute-done | bytes 2359328 | tf_op jit(solution)/shard_map/ppermute | solution.py:284
  388.4 2.7 add_convert_fusion.2
  396.3 45.4 %collective-permute-done.15 = bf16[4,3,64,512]{3,2,1,0:T(8,128)(2,1)} collective-permute-done((bf16[4,3,64,512]{3,2,1,0:T(8,128)(2,1)}, bf16[4,3,64,512]{3,2,1,0:T(8,128)(2,1)}, u32[]{:S(2)}, u32[]{:S(2)}) %collective-permute-start.15) | collective-permute-done | bytes 786464 | tf_op jit(solution)/shard_map/ppermute | solution.py:284
  452.9 8.2 %input_back.1 = (f32[1024,1024]{1,0:T(8,128)}, f32[1,1024]{1,0:T(1,128)}) custom-call(f32[1024,1024]{1,0:T(8,128)} %get-tuple-element.123.own, bf16[1024,1024]{1,0:T(8,128)(2,1)} %collective-permute-done.19.other, bf16[1024,1024]{1,0:T(8,128)(2,1)} %tokens.5, f32[1,1024]{1,0:T(1,128)} %bitcast.81, f32[1024,1024]{1,0:T(8,128)} %get-tuple-element.125.grad_middle), custom_call_target="tpu_custom_call" | custom-call | bytes 16777216 | tf_op jit(solution)/shard_map/input_back/pallas_call | solution.py:504
  463.1 3.4 collective-permute-start.22
  470.1 4.2 add_convert_fusion.1
  474.3 6.7 %collective-permute-done.24 = f32[1,3584]{1,0:T(1,128)S(1)} collective-permute-done((f32[1,3584]{1,0:T(1,128)S(1)}, f32[1,3584]{1,0:T(1,128)S(1)}, u32[]{:S(2)}, u32[]{:S(2)}) %collective-permute-start.24) | collective-permute-done | bytes 14368 | tf_op jit(solution)/shard_map/ppermute | solution.py:284
  481.4 11.5 %collective-permute-done.22 = bf16[2,3,64,1280]{3,2,1,0:T(8,128)(2,1)S(1)} collective-permute-done((bf16[2,3,64,1280]{3,2,1,0:T(8,128)(2,1)S(1)}, bf16[2,3,64,1280]{3,2,1,0:T(8,128)(2,1)S(1)}, u32[]{:S(2)}, u32[]{:S(2)}) %collective-permute-start.22) | collective-permute-done | bytes 983072 | tf_op jit(solution)/shard_map/ppermute | solution.py:293
  495.0 8.1 %collective-permute-start.26 = (bf16[2,4,64,512]{3,2,1,0:T(8,128)(2,1)S(1)}, bf16[2,4,64,512]{3,2,1,0:T(8,128)(2,1)}, u32[]{:S(2)}, u32[]{:S(2)}) collective-permute-start(bf16[2,4,64,512]{3,2,1,0:T(8,128)(2,1)S(1)} %get-tuple-element.171), channel_id=1, source_target_pairs={{0,8},{2,10},{4,12},{6,14},{24,16},{26,18},{28,20},{30,22},{1,9},{... | collective-permute-start | bytes 1572872 | tf_op jit(solution)/shard_map/ppermute | solution.py:293
  503.1 10.0 %collective-permute-done.28 = f32[1,3584]{1,0:T(1,128)S(1)} collective-permute-done((f32[1,3584]{1,0:T(1,128)S(1)}, f32[1,3584]{1,0:T(1,128)S(1)}, u32[]{:S(2)}, u32[]{:S(2)}) %collective-permute-start.28) | collective-permute-done | bytes 14368 | tf_op jit(solution)/shard_map/ppermute | solution.py:284
  516.6 6.6 %collective-permute-start.30 = (bf16[3,64,1280]{2,1,0:T(8,128)(2,1)S(1)}, bf16[3,64,1280]{2,1,0:T(8,128)(2,1)S(1)}, u32[]{:S(2)}, u32[]{:S(2)}) collective-permute-start(bf16[3,64,1280]{2,1,0:T(8,128)(2,1)S(1)} %dynamic-slice_bitcast_fusion.4), channel_id=1, source_target_pairs={{0,8},{2,10},{4,12},{6,14},{8,0},{10,2},{12,4},{14,6},{16,24},{18,... | collective-permute-start | bytes 1474568 | tf_op jit(solution)/shard_map/ppermute | solution.py:284
  523.9 2.8 collective-permute-start.31
  526.7 11.4 %collective-permute-done.31 = f32[1,3584]{1,0:T(1,128)S(1)} collective-permute-done((f32[1,3584]{1,0:T(1,128)S(1)}, f32[1,3584]{1,0:T(1,128)S(1)}, u32[]{:S(2)}, u32[]{:S(2)}) %collective-permute-start.31) | collective-permute-done | bytes 14368 | tf_op jit(solution)/shard_map/ppermute | solution.py:284
  540.5 4.3 collective-permute-done.33
  (162 shorter events, 67.0 us)
Async XLA Ops:
  7.2 177.0 %all-gather.7.cloned.1.call-start = ((), (), s32[]{:S(2)}) async-start(), calls=%async_computation.3 | async-start | bytes 6684672 | tf_op jit(solution)/shard_map/all_gather | solution.py:900
  10.1 227.8 %all-gather.5.cloned.1.call-start = ((), (), s32[]{:S(2)}) async-start(), calls=%async_computation.2 | async-start | bytes 8355840 | tf_op jit(solution)/shard_map/all_gather | solution.py:901
  11.1 535.3 %reduce-scatter.2.cloned.1.call-start = ((), (), s32[]{:S(2)}) async-start(), calls=%async_computation.1 | async-start | bytes 6684672 | tf_op jit(solution)/shard_map/reduce_scatter | solution.py:922
  15.4 60.7 %collective-permute-start.3 = (bf16[1024,1024]{1,0:T(8,128)(2,1)}, bf16[1024,1024]{1,0:T(8,128)(2,1)}, u32[]{:S(2)}, u32[]{:S(2)}) collective-permute-start(bf16[1024,1024]{1,0:T(8,128)(2,1)} %norm.1.own), channel_id=1, source_target_pairs={{0,1},{1,0},{2,3},{3,2},{4,5},{5,4},{6,7},{7,6},{8,9},{9,8},{10,11... | collective-permute-start | bytes 6291464 | tf_op jit(solution)/shard_map/ppermute | solution.py:280
  15.9 10.5 %collective-permute-start = (bf16[4,64,512]{2,1,0:T(8,128)(2,1)S(1)}, bf16[4,64,512]{2,1,0:T(8,128)(2,1)S(1)}, u32[]{:S(2)}, u32[]{:S(2)}) collective-permute-start(bf16[4,64,512]{2,1,0:T(8,128)(2,1)S(1)} %get-tuple-element.178), channel_id=1, source_target_pairs={{0,8},{2,10},{4,12},{6,14},{8,0},{10,2},{12,4},{14,6},{16,24},{18,... | collective-permute-start | bytes 786440 | tf_op jit(solution)/shard_map/ppermute | solution.py:284
  27.2 61.3 %collective-permute-start.6 = (bf16[1024,1024]{1,0:T(8,128)(2,1)S(1)}, bf16[1024,1024]{1,0:T(8,128)(2,1)}, u32[]{:S(2)}, u32[]{:S(2)}) collective-permute-start(bf16[1024,1024]{1,0:T(8,128)(2,1)S(1)} %copy-done.1), channel_id=1, source_target_pairs={{0,1},{1,0},{2,3},{3,2},{4,5},{5,4},{6,7},{7,6},{8,9},{9,8},{10,11... | collective-permute-start | bytes 6291464 | tf_op jit(solution)/shard_map/ppermute | solution.py:280
  27.4 47.3 %collective-permute-start.2 = (bf16[2,4,64,512]{3,2,1,0:T(8,128)(2,1)S(1)}, bf16[2,4,64,512]{3,2,1,0:T(8,128)(2,1)S(1)}, u32[]{:S(2)}, u32[]{:S(2)}) collective-permute-start(bf16[2,4,64,512]{3,2,1,0:T(8,128)(2,1)S(1)} %collective-permute-done.1), channel_id=1, source_target_pairs={{8,0},{10,2},{12,4},{14,6},{16,24},{18,26},{20,28},{22,30},{9,1},{... | collective-permute-start | bytes 1572872 | tf_op jit(solution)/shard_map/ppermute | solution.py:293
  85.5 24.1 %collective-permute-start.5 = (bf16[4,2,64,512]{3,2,1,0:T(8,128)(2,1)}, bf16[4,2,64,512]{3,2,1,0:T(8,128)(2,1)S(1)}, u32[]{:S(2)}, u32[]{:S(2)}) collective-permute-start(bf16[4,2,64,512]{3,2,1,0:T(8,128)(2,1)} %get-tuple-element.175), channel_id=1, source_target_pairs={{0,2},{2,0},{4,6},{6,4},{8,10},{10,8},{12,14},{14,12},{16,18},{18,... | collective-permute-start | bytes 1572872 | tf_op jit(solution)/shard_map/ppermute | solution.py:284
  87.1 22.8 %collective-permute-start.4 = (bf16[4,2,64,512]{3,2,1,0:T(8,128)(2,1)}, bf16[4,2,64,512]{3,2,1,0:T(8,128)(2,1)S(1)}, u32[]{:S(2)}, u32[]{:S(2)}) collective-permute-start(bf16[4,2,64,512]{3,2,1,0:T(8,128)(2,1)} %get-tuple-element.176), channel_id=1, source_target_pairs={{0,4},{2,6},{4,0},{6,2},{8,12},{10,14},{12,8},{14,10},{16,20},{18,... | collective-permute-start | bytes 1572872 | tf_op jit(solution)/shard_map/ppermute | solution.py:284
  110.1 24.9 %collective-permute-start.7 = (bf16[2,4,2,64,512]{4,3,2,1,0:T(8,128)(2,1)S(1)}, bf16[2,4,2,64,512]{4,3,2,1,0:T(8,128)(2,1)S(1)}, u32[]{:S(2)}, u32[]{:S(2)}) collective-permute-start(bf16[2,4,2,64,512]{4,3,2,1,0:T(8,128)(2,1)S(1)} %maximum_select_fusion.1.first_own), channel_id=1, source_target_pairs={{0,2},{2,0},{4,6},{6,4},{8,10},{10,8},{12,14},{14,12},{16,18},{18,... | collective-permute-start | bytes 3145736 | tf_op jit(solution)/shard_map/ppermute | solution.py:284
  111.4 24.5 %collective-permute-start.8 = (bf16[2,4,2,64,512]{4,3,2,1,0:T(8,128)(2,1)S(1)}, bf16[2,4,2,64,512]{4,3,2,1,0:T(8,128)(2,1)}, u32[]{:S(2)}, u32[]{:S(2)}) collective-permute-start(bf16[2,4,2,64,512]{4,3,2,1,0:T(8,128)(2,1)S(1)} %maximum_select_fusion.2.second_own), channel_id=1, source_target_pairs={{0,4},{2,6},{4,0},{6,2},{8,12},{10,14},{12,8},{14,10},{16,20},{18,... | collective-permute-start | bytes 3145736 | tf_op jit(solution)/shard_map/ppermute | solution.py:284
  317.7 4.5 collective-permute-start.14
  318.1 67.7 %collective-permute-start.12 = (bf16[2,4,3,64,768]{4,3,2,1,0:T(8,128)(2,1)}, bf16[2,4,3,64,768]{4,3,2,1,0:T(8,128)(2,1)S(1)}, u32[]{:S(2)}, u32[]{:S(2)}) collective-permute-start(bf16[2,4,3,64,768]{4,3,2,1,0:T(8,128)(2,1)} %get-tuple-element.99), channel_id=1, source_target_pairs={{0,4},{2,6},{4,0},{6,2},{8,12},{10,14},{12,8},{14,10},{16,20},{18,... | collective-permute-start | bytes 7077896 | tf_op jit(solution)/shard_map/ppermute | solution.py:284
  319.7 46.1 %collective-permute-start.11 = (bf16[2,4,3,64,512]{4,3,2,1,0:T(8,128)(2,1)}, bf16[2,4,3,64,512]{4,3,2,1,0:T(8,128)(2,1)}, u32[]{:S(2)}, u32[]{:S(2)}) collective-permute-start(bf16[2,4,3,64,512]{4,3,2,1,0:T(8,128)(2,1)} %get-tuple-element.98), channel_id=1, source_target_pairs={{0,2},{2,0},{4,6},{6,4},{8,10},{10,8},{12,14},{14,12},{16,18},{18,... | collective-permute-start | bytes 4718600 | tf_op jit(solution)/shard_map/ppermute | solution.py:284
  385.8 67.1 %collective-permute-start.19 = (bf16[1024,1024]{1,0:T(8,128)(2,1)}, bf16[1024,1024]{1,0:T(8,128)(2,1)}, u32[]{:S(2)}, u32[]{:S(2)}) collective-permute-start(bf16[1024,1024]{1,0:T(8,128)(2,1)} %get-tuple-element.124), channel_id=1, source_target_pairs={{0,1},{1,0},{2,3},{3,2},{4,5},{5,4},{6,7},{7,6},{8,9},{9,8},{10,11... | collective-permute-start | bytes 6291464 | tf_op jit(solution)/shard_map/ppermute | solution.py:280
  385.8 58.6 %collective-permute-start.18 = (bf16[2,4,2,64,512]{4,3,2,1,0:T(8,128)(2,1)}, bf16[2,4,2,64,512]{4,3,2,1,0:T(8,128)(2,1)}, u32[]{:S(2)}, u32[]{:S(2)}) collective-permute-start(bf16[2,4,2,64,512]{4,3,2,1,0:T(8,128)(2,1)} %get-tuple-element.122), channel_id=1, source_target_pairs={{0,4},{2,6},{4,0},{6,2},{8,12},{10,14},{12,8},{14,10},{16,20},{18,... | collective-permute-start | bytes 3145736 | tf_op jit(solution)/shard_map/ppermute | solution.py:284
  387.4 59.6 %collective-permute-start.17 = (bf16[2,4,2,64,512]{4,3,2,1,0:T(8,128)(2,1)}, bf16[2,4,2,64,512]{4,3,2,1,0:T(8,128)(2,1)}, u32[]{:S(2)}, u32[]{:S(2)}) collective-permute-start(bf16[2,4,2,64,512]{4,3,2,1,0:T(8,128)(2,1)} %get-tuple-element.120), channel_id=1, source_target_pairs={{0,2},{2,0},{4,6},{6,4},{8,10},{10,8},{12,14},{14,12},{16,18},{18,... | collective-permute-start | bytes 3145736 | tf_op jit(solution)/shard_map/ppermute | solution.py:284
  392.2 49.6 %collective-permute-start.15 = (bf16[4,3,64,512]{3,2,1,0:T(8,128)(2,1)}, bf16[4,3,64,512]{3,2,1,0:T(8,128)(2,1)}, u32[]{:S(2)}, u32[]{:S(2)}) collective-permute-start(bf16[4,3,64,512]{3,2,1,0:T(8,128)(2,1)} %dynamic-slice_bitcast_fusion.1), channel_id=1, source_target_pairs={{0,4},{2,6},{4,0},{6,2},{8,12},{10,14},{12,8},{14,10},{16,20},{18,... | collective-permute-start | bytes 2359304 | tf_op jit(solution)/shard_map/ppermute | solution.py:284
  395.6 55.6 %collective-permute-start.16 = (bf16[4,3,64,768]{3,2,1,0:T(8,128)(2,1)S(1)}, bf16[4,3,64,768]{3,2,1,0:T(8,128)(2,1)}, u32[]{:S(2)}, u32[]{:S(2)}) collective-permute-start(bf16[4,3,64,768]{3,2,1,0:T(8,128)(2,1)S(1)} %dynamic-slice_bitcast_fusion), channel_id=1, source_target_pairs={{0,2},{2,0},{4,6},{6,4},{8,10},{10,8},{12,14},{14,12},{16,18},{18,... | collective-permute-start | bytes 3538952 | tf_op jit(solution)/shard_map/ppermute | solution.py:284
  441.8 28.3 %collective-permute-start.25 = (bf16[1024,1024]{1,0:T(8,128)(2,1)}, bf16[1024,1024]{1,0:T(8,128)(2,1)}, u32[]{:S(2)}, u32[]{:S(2)}) collective-permute-start(bf16[1024,1024]{1,0:T(8,128)(2,1)} %get-tuple-element.135), channel_id=1, source_target_pairs={{0,1},{1,0},{2,3},{3,2},{4,5},{5,4},{6,7},{7,6},{8,9},{9,8},{10,11... | collective-permute-start | bytes 6291464 | tf_op jit(solution)/shard_map/ppermute | solution.py:280
  461.8 6.9 %collective-permute-start.23 = (f32[1,3584]{1,0:T(1,128)S(1)}, f32[1,3584]{1,0:T(1,128)S(1)}, u32[]{:S(2)}, u32[]{:S(2)}) collective-permute-start(f32[1,3584]{1,0:T(1,128)S(1)} %pad_maximum_fusion.3), channel_id=1, source_target_pairs={{0,2},{2,0},{4,6},{6,4},{8,10},{10,8},{12,14},{14,12},{16,18},{18,... | collective-permute-start | bytes 43016 | tf_op jit(solution)/shard_map/ppermute | solution.py:284
  463.1 29.7 %collective-permute-start.22 = (bf16[2,3,64,1280]{3,2,1,0:T(8,128)(2,1)S(1)}, bf16[2,3,64,1280]{3,2,1,0:T(8,128)(2,1)S(1)}, u32[]{:S(2)}, u32[]{:S(2)}) collective-permute-start(bf16[2,3,64,1280]{3,2,1,0:T(8,128)(2,1)S(1)} %get-tuple-element.169), channel_id=1, source_target_pairs={{0,8},{2,10},{4,12},{6,14},{24,16},{26,18},{28,20},{30,22},{1,9},{... | collective-permute-start | bytes 2949128 | tf_op jit(solution)/shard_map/ppermute | solution.py:293
  466.7 14.4 %collective-permute-start.21 = (bf16[4,2,64,512]{3,2,1,0:T(8,128)(2,1)S(1)}, bf16[4,2,64,512]{3,2,1,0:T(8,128)(2,1)S(1)}, u32[]{:S(2)}, u32[]{:S(2)}) collective-permute-start(bf16[4,2,64,512]{3,2,1,0:T(8,128)(2,1)S(1)} %dynamic-slice_bitcast_fusion.2), channel_id=1, source_target_pairs={{0,2},{2,0},{4,6},{6,4},{8,10},{10,8},{12,14},{14,12},{16,18},{18,... | collective-permute-start | bytes 1572872 | tf_op jit(solution)/shard_map/ppermute | solution.py:284
  467.9 13.3 %collective-permute-start.20 = (bf16[4,2,64,512]{3,2,1,0:T(8,128)(2,1)S(1)}, bf16[4,2,64,512]{3,2,1,0:T(8,128)(2,1)S(1)}, u32[]{:S(2)}, u32[]{:S(2)}) collective-permute-start(bf16[4,2,64,512]{3,2,1,0:T(8,128)(2,1)S(1)} %dynamic-slice_bitcast_fusion.3), channel_id=1, source_target_pairs={{0,4},{2,6},{4,0},{6,2},{8,12},{10,14},{12,8},{14,10},{16,20},{18,... | collective-permute-start | bytes 1572872 | tf_op jit(solution)/shard_map/ppermute | solution.py:284
  468.7 12.3 %collective-permute-start.24 = (f32[1,3584]{1,0:T(1,128)S(1)}, f32[1,3584]{1,0:T(1,128)S(1)}, u32[]{:S(2)}, u32[]{:S(2)}) collective-permute-start(f32[1,3584]{1,0:T(1,128)S(1)} %add.145), channel_id=1, source_target_pairs={{0,4},{2,6},{4,0},{6,2},{8,12},{10,14},{12,8},{14,10},{16,20},{18,... | collective-permute-start | bytes 43016 | tf_op jit(solution)/shard_map/ppermute | solution.py:284
  493.1 22.0 %collective-permute-start.27 = (bf16[2,3,64,1280]{3,2,1,0:T(8,128)(2,1)S(1)}, bf16[2,3,64,1280]{3,2,1,0:T(8,128)(2,1)}, u32[]{:S(2)}, u32[]{:S(2)}) collective-permute-start(bf16[2,3,64,1280]{3,2,1,0:T(8,128)(2,1)S(1)} %add_convert_fusion.6), channel_id=1, source_target_pairs={{8,16},{10,18},{12,20},{14,22},{16,8},{18,10},{20,12},{22,14},{9,1... | collective-permute-start | bytes 2949128 | tf_op jit(solution)/shard_map/ppermute | solution.py:293
  495.0 18.2 %collective-permute-start.26 = (bf16[2,4,64,512]{3,2,1,0:T(8,128)(2,1)S(1)}, bf16[2,4,64,512]{3,2,1,0:T(8,128)(2,1)}, u32[]{:S(2)}, u32[]{:S(2)}) collective-permute-start(bf16[2,4,64,512]{3,2,1,0:T(8,128)(2,1)S(1)} %get-tuple-element.171), channel_id=1, source_target_pairs={{0,8},{2,10},{4,12},{6,14},{24,16},{26,18},{28,20},{30,22},{1,9},{... | collective-permute-start | bytes 1572872 | tf_op jit(solution)/shard_map/ppermute | solution.py:293
  503.1 10.0 %collective-permute-start.28 = (f32[1,3584]{1,0:T(1,128)S(1)}, f32[1,3584]{1,0:T(1,128)S(1)}, u32[]{:S(2)}, u32[]{:S(2)}) collective-permute-start(f32[1,3584]{1,0:T(1,128)S(1)} %add.146), channel_id=1, source_target_pairs={{0,8},{2,10},{4,12},{6,14},{8,0},{10,2},{12,4},{14,6},{16,24},{18,... | collective-permute-start | bytes 43016 | tf_op jit(solution)/shard_map/ppermute | solution.py:284
  516.6 21.5 %collective-permute-start.30 = (bf16[3,64,1280]{2,1,0:T(8,128)(2,1)S(1)}, bf16[3,64,1280]{2,1,0:T(8,128)(2,1)S(1)}, u32[]{:S(2)}, u32[]{:S(2)}) collective-permute-start(bf16[3,64,1280]{2,1,0:T(8,128)(2,1)S(1)} %dynamic-slice_bitcast_fusion.4), channel_id=1, source_target_pairs={{0,8},{2,10},{4,12},{6,14},{8,0},{10,2},{12,4},{14,6},{16,24},{18,... | collective-permute-start | bytes 1474568 | tf_op jit(solution)/shard_map/ppermute | solution.py:284
  523.2 15.0 %collective-permute-start.29 = (bf16[2,4,64,512]{3,2,1,0:T(8,128)(2,1)}, bf16[2,4,64,512]{3,2,1,0:T(8,128)(2,1)S(1)}, u32[]{:S(2)}, u32[]{:S(2)}) collective-permute-start(bf16[2,4,64,512]{3,2,1,0:T(8,128)(2,1)} %add_convert_fusion.8), channel_id=1, source_target_pairs={{8,16},{10,18},{12,20},{14,22},{16,8},{18,10},{20,12},{22,14},{9,1... | collective-permute-start | bytes 1572872 | tf_op jit(solution)/shard_map/ppermute | solution.py:293
  523.9 14.2 %collective-permute-start.31 = (f32[1,3584]{1,0:T(1,128)S(1)}, f32[1,3584]{1,0:T(1,128)S(1)}, u32[]{:S(2)}, u32[]{:S(2)}) collective-permute-start(f32[1,3584]{1,0:T(1,128)S(1)} %add.151), channel_id=1, source_target_pairs={{0,16},{2,18},{4,20},{6,22},{8,24},{10,26},{12,28},{14,30},{16,0},... | collective-permute-start | bytes 43016 | tf_op jit(solution)/shard_map/ppermute | solution.py:284
  538.4 6.4 %collective-permute-start.33 = (bf16[4,64,512]{2,1,0:T(8,128)(2,1)S(1)}, bf16[4,64,512]{2,1,0:T(8,128)(2,1)S(1)}, u32[]{:S(2)}, u32[]{:S(2)}) collective-permute-start(bf16[4,64,512]{2,1,0:T(8,128)(2,1)S(1)} %dynamic-slice_bitcast_fusion.5), channel_id=1, source_target_pairs={{0,8},{2,10},{4,12},{6,14},{8,0},{10,2},{12,4},{14,6},{16,24},{18,... | collective-permute-start | bytes 786440 | tf_op jit(solution)/shard_map/ppermute | solution.py:284
  (30 other events, 250.8 us)
Sparse Core Ops, SparseCore 0:
  11.4 113.6 all-gather.6
  127.8 106.3 all-gather.4
  318.2 163.4 reduce-scatter.1

commit v3 on v2

--- a/solution.py
+++ b/solution.py
@@ -541,11 +541,13 @@
             send[side, z, at] = product[kind, z, pl.ds(1 - bits[1], 1), side][0]
 
 
-def ffn_kernel(bits, normed, cotangent, normed_t, cotangent_t, shards, *rest, pairs, carried):
+def ffn_kernel(
+    bits, normed, cotangent, normed_t, cotangent_t, shards, *rest, pairs, carried, final
+):
     if carried:
         carry_in, rest = rest[:2], rest[2:]
     outs, rest = rest[: 4 if pairs else 1], rest[4 if pairs else 1 :]
-    totals_out, scratch = rest[: 4 if pairs else 2], rest[4 if pairs else 2 :]
+    totals_out, scratch = rest[: 4 if final else 2], rest[4 if final else 2 :]
     weights, made, totals, product, narrowed, sems = scratch
     step, last = pl.program_id(0), pl.num_programs(0) - 1
     tokens, width = normed.shape
@@ -554,7 +556,7 @@
     loads = []
     if carried:
         loads = [pltpu.make_async_copy(carry_in[i], totals.at[i], sems.at[i]) for i in range(2)]
-    if pairs:
+    if final:
         saves = [
             pltpu.make_async_copy(totals.at[i, pl.ds(0, own)], totals_out[i], sems.at[i])
             for i in range(2)
@@ -601,7 +603,7 @@
 
     @pl.when(step == last)
     def _():
-        if pairs:
+        if final:
             narrowed[...] = narrow(totals[:, own:])
         for copy in saves:
             copy.start()
@@ -634,7 +636,7 @@
             copy.wait()
 
 
-def ffn_call(bits, rows, rows_t, shards, pairs=False, carry=()):
+def ffn_call(bits, rows, rows_t, shards, pairs, carry=()):
     tokens, width = rows[0].shape
     places, _, shard, units = shards.shape
     tiles = units // TILE
@@ -653,17 +655,22 @@
         second_spec = pl.BlockSpec(
             piece + (TILE,), lambda i, b: (0, 0, 0, 0, jnp.maximum(i - first_tiles, 0))
         )
-        out_specs = [first_spec] * 2 + [second_spec] * 2 + [anywhere] * 4
+        out_specs = [first_spec] * 2 + [second_spec] * 2
         first_shape = shape(*piece, first_tiles * TILE)
         second_shape = shape(*piece, units - first_tiles * TILE)
         out_shape = [first_shape] * 2 + [second_shape] * 2
+    else:
+        first_tiles = 0
+        out_specs = [natural]
+        out_shape = [shape(*shards.shape)]
+    final = bool(carry)
+    if final:
         out_shape += [shape(own, width, dtype=jnp.float32)] * 2 + [shape(own, width)] * 2
     else:
-        first_tiles = 0
-        out_specs = [natural] + [anywhere] * 2
-        out_shape = [shape(*shards.shape)] + [shape(tokens, width, dtype=jnp.float32)] * 2
+        out_shape += [shape(tokens, width, dtype=jnp.float32)] * 2
+    out_specs += [anywhere] * (4 if final else 2)
     return pl.pallas_call(
-        functools.partial(ffn_kernel, pairs=first_tiles, carried=bool(carry)),
+        functools.partial(ffn_kernel, pairs=first_tiles, carried=final, final=final),
         out_shape=out_shape,
         grid_spec=pltpu.PrefetchScalarGridSpec(
             num_scalar_prefetch=1,
@@ -675,7 +682,7 @@
                 pltpu.VMEM((3, tokens, TILE), jnp.bfloat16),
                 pltpu.VMEM((2, tokens, width), jnp.float32),
                 pltpu.VMEM((3, 4, 2, 2, shard, TILE), jnp.bfloat16),
-                pltpu.VMEM((2, own, width) if pairs else (2, 16, 128), jnp.bfloat16),
+                pltpu.VMEM((2, own, width) if final else (2, 16, 128), jnp.bfloat16),
                 pltpu.SemaphoreType.DMA((4,)),
             ],
         ),
@@ -887,7 +894,7 @@
     out_grad,
 ):
     rows, width = tokens.shape
-    split = down_weight.shape[1] // (2 * TILE) * TILE
+    split = (down_weight.shape[1] // TILE + 1) // 2 * TILE
     collect = lambda values: both_call(values, exchange(values))
     bits = jnp.stack(place_bits()[:0:-1]).astype(jnp.int32)
     gain1, gain2 = norm_gain1[None], norm_gain2[None]
@@ -899,18 +906,21 @@
     big = jnp.concatenate([jnp.transpose(gate_up_weight, (1, 0, 2)), down_weight[None]], 0)
     big1 = lax.all_gather(big[..., :split], "dp", axis=0)
     big2 = lax.all_gather(big[..., split:], "dp", axis=0)
-
     near = line_near(small)
     (normed1,) = row_call(norm_kernel, "norm", (tokens, gain1), (narrow_rows,))
-    group_n1, normed1_t = collect(normed1)
     lines = line_far(near, line_middle(near))
-    lines, group_n1 = tie(lines, group_n1)
+    normed1_other, out_grad_other = exchange(normed1), exchange(out_grad)
     s_first, s_second = gather_pair(lines[:, :2], 2), gather_pair(lines[:, 2:], 1)
-    group_grad, cotangent_t = collect(out_grad)
-    s_first, s_second, group_grad, cotangent_t, normed1_t = tie(
-        s_first, s_second, group_grad, cotangent_t, normed1_t
-    )
-    s_first, s_second = (s_first, across(s_first, 1)), (s_second, across(s_second, 2))
+    s_first, s_second, normed1_other, out_grad_other = tie(
+        s_first, s_second, normed1_other, out_grad_other
+    )
+    s_other, s_otherb = across(s_first, 1), across(s_second, 2)
+    group_n1, normed1_t = both_call(normed1, normed1_other)
+    group_grad, cotangent_t = both_call(out_grad, out_grad_other)
+    s_other, s_otherb, group_n1, normed1_t, group_grad, cotangent_t = tie(
+        s_other, s_otherb, group_n1, normed1_t, group_grad, cotangent_t
+    )
+    s_first, s_second = (s_first, s_other), (s_second, s_otherb)
     saved, mixer_weights, own, other = mixer_call(bits, group_n1, conv_kernel, s_first, s_second)
     middle, normed2 = row_call(
         middle_kernel, "middle", (tokens, own, exchange(other), gain2), (wide_rows, narrow_rows)
@@ -918,13 +928,20 @@
     group_n2, normed2_t = collect(normed2)
     rows_both, rows_t = (group_n2, group_grad), (normed2_t, cotangent_t)
 
-    grads1, *carry = ffn_call(bits, rows_both, rows_t, big1)
-    grads1 = lax.psum_scatter(grads1, "dp", scatter_dimension=0)
-    send2, keep2, send2b, keep2b, forward, backward, forward_other, backward_other = ffn_call(
-        bits, rows_both, rows_t, big2, True, tuple(carry)
-    )
+    send1, keep1, send1b, keep1b, *carry = ffn_call(bits, rows_both, rows_t, big1, True)
+    took1, took1b = across(send1, 1), across(send1b, 2)
+    grads2, forward, backward, forward_other, backward_other = ffn_call(
+        bits, rows_both, rows_t, big2, False, tuple(carry)
+    )
+    took1, took1b, grads2, forward, backward, forward_other, backward_other = tie(
+        took1, took1b, grads2, forward, backward, forward_other, backward_other
+    )
+    grads2 = lax.psum_scatter(grads2, "dp", scatter_dimension=0)
     backward_other = exchange(backward_other)
-    took2, took2b = across(send2, 1), across(send2b, 2)
+    first1, second1 = narrow(add_wide(keep1, took1)), narrow(add_wide(keep1b, took1b))
+    y_bit, x_bit = place_bits()[1:]
+    keep1, keep1b = pick(first1, y_bit), pick(second1, x_bit)
+    took1, took1b = across(pick(first1, 1 - y_bit), 2), across(pick(second1, 1 - x_bit), 1)
     grad_middle, narrowed, gain_two_grad = row_call(
         middle_back_kernel,
         "middle_back",
@@ -935,14 +952,13 @@
     s_send, s_keep, s_sendb, s_keepb, own, other, kernel_grad = mixer_back_call(
         bits, group_gm, grads_t, normed1_t, conv_kernel, saved, mixer_weights
     )
-    took2, took2b, s_send, s_keep, s_sendb, s_keepb, own, other, kernel_grad = tie(
-        took2, took2b, s_send, s_keep, s_sendb, s_keepb, own, other, kernel_grad
-    )
-
-    first2, second2 = narrow(add_wide(keep2, took2)), narrow(add_wide(keep2b, took2b))
-    first2, second2 = reduce_pair(first2, 2), reduce_pair(second2, 1)
-    s_first = narrow(add_wide(s_keep, across(s_send, 1)))
-    s_second = narrow(add_wide(s_keepb, across(s_sendb, 2)))
+    took1, took1b, s_send, s_keep, s_sendb, s_keepb, own, other, kernel_grad = tie(
+        took1, took1b, s_send, s_keep, s_sendb, s_keepb, own, other, kernel_grad
+    )
+
+    first1, second1 = narrow(add_wide(keep1, took1)), narrow(add_wide(keep1b, took1b))
+    s_took, s_tookb = across(s_send, 1), across(s_sendb, 2)
+    mine1, theirs1 = reduce_far(jnp.concatenate([first1, second1], -1))
     input_grad, gain_one_grad = row_call(
         input_back_kernel,
         "input_back",
@@ -950,29 +966,28 @@
         (wide_rows, gain_row),
     )
     summed = jnp.concatenate([gain_one_grad, gain_two_grad, kernel_grad.reshape(1, -1)], 1)
-    first2, second2, s_first, s_second, summed = tie(first2, second2, s_first, s_second, summed)
+    s_took, s_tookb, mine1, theirs1, summed = tie(s_took, s_tookb, mine1, theirs1, summed)
+    s_first, s_second = narrow(add_wide(s_keep, s_took)), narrow(add_wide(s_keepb, s_tookb))
 
     s_first, s_second = reduce_pair(s_first, 2), reduce_pair(s_second, 1)
-    mine2, theirs2 = reduce_far(jnp.concatenate([first2, second2], -1))
+    mine1 = reduce_middle(mine1, theirs1)
     result = narrow(middle + (forward + exchange(forward_other).astype(jnp.float32)))
     summed = summed + across(summed, 1)
     summed = summed + across(summed, 2)
-    s_first, s_second, mine2, theirs2, summed, result = tie(
-        s_first, s_second, mine2, theirs2, summed, result
-    )
-
+    s_first, s_second, mine1, summed, result = tie(s_first, s_second, mine1, summed, result)
+
+    grads2, s_first, s_second = tie(grads2, s_first, s_second)
     mine_s, theirs_s = reduce_far(jnp.concatenate([s_first, s_second], 1))
-    mine2 = reduce_middle(mine2, theirs2)
+    grads1 = reduce_near(mine1)
     summed = summed + across(summed, 4)
-    mine_s, theirs_s, mine2, summed = tie(mine_s, theirs_s, mine2, summed)
-    grads2 = reduce_near(mine2)
+    mine_s, theirs_s, grads1, summed = tie(mine_s, theirs_s, grads1, summed)
     mine_s = reduce_middle(mine_s, theirs_s)
     summed = summed + across(summed, 8)
-    mine_s, grads2, summed = tie(mine_s, grads2, summed)
+    mine_s, summed = tie(mine_s, summed)
     small_grads = reduce_near(mine_s)
     gains = summed[0, : 2 * width]
     gains = gains + exchange(gains)
-    big_grads = jnp.concatenate([grads1.astype(jnp.float32), grads2], -1)
+    big_grads = jnp.concatenate([grads1, grads2.astype(jnp.float32)], -1)
     return (
         result,
         input_grad,

time: 566 us -> 538 us (0.951)
  waiting for transfers between devices: 216 us -> 170 us
  starting transfers between devices: 46 us -> 62.6 us
    ppermute x19, waiting for transfers between devices: 144 us -> 70.6 us  [across(): lax.ppermute(values, 'dp', [(place, place ^ bit) for place in range(16)])]
    ppermute x19, starting transfers between devices: 28.5 us -> 50.6 us  [across(): lax.ppermute(values, 'dp', [(place, place ^ bit) for place in range(16)])]
    reduce_scatter x1, waiting for transfers between devices: 0.01 us -> 15.6 us  [per_device_pairs(): grads2 = lax.psum_scatter(grads2, 'dp', scatter_dimension=0)]
    ppermute x6, waiting for transfers between devices: 57.5 us -> 70.5 us  [between(): return lax.ppermute(values, 'dp', pairs)]
  transfers between devices with their start and end apart: 37 -> 37, of which waited for: 18 -> 17; matrix products, arithmetic and copies ran while one was open for 6% -> 7% of each run, Pallas kernels for 29% -> 45%
where the time goes in v3:
time: 538 us; the launch traced here: 530 us
  Pallas kernels  236 us (44%)
  waiting for transfers between devices  170 us (32%)
  starting transfers between devices  62.6 us (12%)
  other arithmetic  31.8 us (6%)
  between operations  14.8 us (3%)
  local copies, waits for them, and re-layouts  14.5 us (3%)
    pallas_call x2, Pallas kernels, ffn_call(): pl.pallas_call(functools.partial(ffn_kernel, pairs=first_tiles, carried=f...  118 us
    ppermute x19, waiting for transfers between devices, across(): lax.ppermute(values, 'dp', [(place, place ^ bit) for place in range(16)])  70.6 us
    ppermute x6, waiting for transfers between devices, between(): return lax.ppermute(values, 'dp', pairs)  70.5 us
    ppermute x19, starting transfers between devices, across(): lax.ppermute(values, 'dp', [(place, place ^ bit) for place in range(16)])  50.6 us
    pallas_call x1, Pallas kernels, mixer_back_call(): pl.pallas_call(mixer_back_kernel, out_shape=[jax.ShapeDtypeStruct((2, 4,...  35.2 us
    pallas_call x4, Pallas kernels, both_call(): pl.pallas_call(both_kernel, out_shape=[jax.ShapeDtypeStruct((2 * rows, wi...  32.4 us
    pallas_call x4, Pallas kernels, row_call(): pl.pallas_call(kernel, out_shape=[jax.ShapeDtypeStruct(*out) for out in o...  28.2 us
    pallas_call x1, Pallas kernels, mixer_call(): pl.pallas_call(mixer_kernel, out_shape=[jax.ShapeDtypeStruct((3, tokens,...  22.2 us
  transfers between devices with their start and end apart: 37, of which 17 were waited for; matrix products, arithmetic and copies ran while one was open for 7% of the time, Pallas kernels for 45%

profile of v3, /device:TPU:0, one launch (start us, length us, event | category | flops | bytes accessed | tf_op | source)
XLA Modules:
  0.0 529.9 jit_solution(5534204917237018255)
XLA Ops:
  10.3 3.1 collective-permute-start
  13.4 6.3 %collective-permute-done = bf16[4,64,512]{2,1,0:T(8,128)(2,1)S(1)} collective-permute-done((bf16[4,64,512]{2,1,0:T(8,128)(2,1)S(1)}, bf16[4,64,512]{2,1,0:T(8,128)(2,1)S(1)}, u32[]{:S(2)}, u32[]{:S(2)}) %collective-permute-start) | collective-permute-done | bytes 262176 | tf_op jit(solution)/shard_map/ppermute | solution.py:284
  21.3 4.3 norm.1.own
  28.3 51.8 %collective-permute-done.2 = bf16[2,4,64,512]{3,2,1,0:T(8,128)(2,1)} collective-permute-done((bf16[2,4,64,512]{3,2,1,0:T(8,128)(2,1)}, bf16[2,4,64,512]{3,2,1,0:T(8,128)(2,1)}, u32[]{:S(2)}, u32[]{:S(2)}) %collective-permute-start.2) | collective-permute-done | bytes 524320 | tf_op jit(solution)/shard_map/ppermute | solution.py:293
  85.5 19.0 %collective-permute-done.4 = bf16[4,2,64,512]{3,2,1,0:T(8,128)(2,1)} collective-permute-done((bf16[4,2,64,512]{3,2,1,0:T(8,128)(2,1)}, bf16[4,2,64,512]{3,2,1,0:T(8,128)(2,1)}, u32[]{:S(2)}, u32[]{:S(2)}) %collective-permute-start.4) | collective-permute-done | bytes 524320 | tf_op jit(solution)/shard_map/ppermute | solution.py:284
  113.6 8.0 %both.4 = (bf16[2048,1024]{1,0:T(8,128)(2,1)}, bf16[1024,2048]{1,0:T(8,128)(2,1)}) custom-call(bf16[1024,1024]{1,0:T(8,128)(2,1)} %norm.1.own, bf16[1024,1024]{1,0:T(8,128)(2,1)} %collective-permute-done.5.other), custom_call_target="tpu_custom_call" | custom-call | bytes 12582912 | tf_op jit(solution)/shard_map/both/pallas_call | solution.py:476
  121.6 8.1 %both.5 = (bf16[2048,1024]{1,0:T(8,128)(2,1)}, bf16[1024,2048]{1,0:T(8,128)(2,1)}) custom-call(bf16[1024,1024]{1,0:T(8,128)(2,1)} %out_grad.1, bf16[1024,1024]{1,0:T(8,128)(2,1)} %collective-permute-done.6.other), custom_call_target="tpu_custom_call" | custom-call | bytes 12582912 | tf_op jit(solution)/shard_map/both/pallas_call | solution.py:476
  129.6 14.6 %collective-permute-done.7.first_other = bf16[2,4,2,64,512]{4,3,2,1,0:T(8,128)(2,1)S(1)} collective-permute-done((bf16[2,4,2,64,512]{4,3,2,1,0:T(8,128)(2,1)}, bf16[2,4,2,64,512]{4,3,2,1,0:T(8,128)(2,1)S(1)}, u32[]{:S(2)}, u32[]{:S(2)}) %collective-permute-start.7) | collective-permute-done | bytes 1048608 | tf_op jit(solution)/shard_map/ppermute | solution.py:284
  145.8 22.2 %mixer.1 = (f32[3,2048,512]{2,1,0:T(8,128)}, bf16[4,1024,512]{2,1,0:T(8,128)(2,1)}, f32[1024,1024]{1,0:T(8,128)}, bf16[1024,1024]{1,0:T(8,128)(2,1)}) custom-call(s32[2]{0:T(128)} %pad_add_fusion.bits, bf16[2048,1024]{1,0:T(8,128)(2,1)} %get-tuple-element.99.normed, bf16[3,512]{1,0:T(4,128)(2,1)} %taps.3, ...), custom_call_target="tpu_custom_call" | custom-call | flops 8589934592 | bytes 83886080 | tf_op jit(solution)/shard_map/mixer/pallas_call | solution.py:749
  168.1 4.4 collective-permute-done.9.other
  173.8 6.6 %middle.1 = (f32[1024,1024]{1,0:T(8,128)}, bf16[1024,1024]{1,0:T(8,128)(2,1)}) custom-call(bf16[1024,1024]{1,0:T(8,128)(2,1)} %tokens.5, f32[1024,1024]{1,0:T(8,128)} %get-tuple-element.102.own, bf16[1024,1024]{1,0:T(8,128)(2,1)} %copy-done.5, f32[1,1024]{1,0:T(1,128)} %bitcast.75), custom_call_target="tpu_custom_call" | custom-call | bytes 16777216 | tf_op jit(solution)/shard_map/middle/pallas_call | solution.py:504
  180.5 4.2 collective-permute-done.10.other
  186.1 8.2 %both.6 = (bf16[2048,1024]{1,0:T(8,128)(2,1)}, bf16[1024,2048]{1,0:T(8,128)(2,1)}) custom-call(bf16[1024,1024]{1,0:T(8,128)(2,1)} %get-tuple-element.104.own, bf16[1024,1024]{1,0:T(8,128)(2,1)} %copy-done.4), custom_call_target="tpu_custom_call" | custom-call | bytes 12582912 | tf_op jit(solution)/shard_map/both/pallas_call | solution.py:476
  194.3 64.2 %ffn.2 = (bf16[2,4,3,64,512]{4,3,2,1,0:T(8,128)(2,1)}, bf16[2,4,3,64,512]{4,3,2,1,0:T(8,128)(2,1)}, bf16[2,4,3,64,768]{4,3,2,1,0:T(8,128)(2,1)}, bf16[2,4,3,64,7...) custom-call(s32[2]{0:T(128)} %pad_add_fusion.bits, ...), custom_call_target="tpu_custom_call" | custom-call | flops 48318382080 | bytes 83886080 | tf_op jit(solution)/shard_map/ffn/pallas_call | solution.py:672
  260.6 53.8 %ffn.3 = (bf16[16,3,64,1024]{3,2,1,0:T(8,128)(2,1)}, f32[1024,1024]{1,0:T(8,128)}, f32[1024,1024]{1,0:T(8,128)}, bf16[1024,1024]{1,0:T(8,128)(2,1)}, bf16[1024,1024]{1,0:T(8,128)(2,1)}) custom-call(s32[2]{0:T(128)} %pad_add_fusion.bits, bf16[2048,1024]{1,0:T(8,128)(2,1)} %get-tuple-element.105.normed, bf16[2048,1024]{1,0:T(8,128)(2,1)} %get-tuple-element.106.cotangent, ...), custom_call_target="tpu_custom_call" | custom-call | flops 38654705664 | bytes 83886080 | tf_op jit(solution)/shard_map/ffn/pallas_call | solution.py:672
  315.9 4.5 collective-permute-done.15.other
  320.4 8.8 %middle_back.1 = (f32[1024,1024]{1,0:T(8,128)}, bf16[1024,1024]{1,0:T(8,128)(2,1)}, f32[1,1024]{1,0:T(1,128)}) custom-call(f32[1024,1024]{1,0:T(8,128)} %get-tuple-element.122.own, bf16[1024,1024]{1,0:T(8,128)(2,1)} %collective-permute-done.15.other, f32[1024,1024]{1,0:T(8,128)} %get-tuple-element.124.middle, f32[1,1024]{1,0:T(1,128)} %bitcast.76, ...), custom_call_target="tpu_custom_call" | custom-call | bytes 16777216 | tf_op jit(solution)/shard_map/middle_back/pallas_call | solution.py:504
  329.4 3.2 add_convert_fusion
  338.6 8.1 %both.7 = (bf16[2048,1024]{1,0:T(8,128)(2,1)}, bf16[1024,2048]{1,0:T(8,128)(2,1)}) custom-call(bf16[1024,1024]{1,0:T(8,128)(2,1)} %get-tuple-element.125.own, bf16[1024,1024]{1,0:T(8,128)(2,1)} %collective-permute-done.16.other), custom_call_target="tpu_custom_call" | custom-call | bytes 12582912 | tf_op jit(solution)/shard_map/both/pallas_call | solution.py:476
  346.7 35.2 %mixer_back.1 = (bf16[2,4,2,64,512]{4,3,2,1,0:T(8,128)(2,1)}, bf16[2,4,2,64,512]{4,3,2,1,0:T(8,128)(2,1)}, bf16[2,4,2,64,512]{4,3,2,1,0:T(8,128)(2,1)}, bf16[2,4...) custom-call(s32[2]{0:T(128)} %pad_add_fusion.bits, ...), custom_call_target="tpu_custom_call" | custom-call | flops 19327352832 | bytes 83886080 | tf_op jit(solution)/shard_map/mixer_back/pallas_call | solution.py:846
  389.7 18.7 %collective-permute-done.19 = bf16[2,3,64,1280]{3,2,1,0:T(8,128)(2,1)S(1)} collective-permute-done((bf16[2,3,64,1280]{3,2,1,0:T(8,128)(2,1)S(1)}, bf16[2,3,64,1280]{3,2,1,0:T(8,128)(2,1)S(1)}, u32[]{:S(2)}, u32[]{:S(2)}) %collective-permute-start.19) | collective-permute-done | bytes 983072 | tf_op jit(solution)/shard_map/ppermute | solution.py:293
  409.6 8.4 %input_back.1 = (f32[1024,1024]{1,0:T(8,128)}, f32[1,1024]{1,0:T(1,128)}) custom-call(f32[1024,1024]{1,0:T(8,128)} %get-tuple-element.143.own, bf16[1024,1024]{1,0:T(8,128)(2,1)} %collective-permute-done.20.other, bf16[1024,1024]{1,0:T(8,128)(2,1)} %tokens.5, f32[1,1024]{1,0:T(1,128)} %bitcast.78, f32[1024,1024]{1,0:T(8,128)} %get-tuple-element.145.grad_middle), custom_call_target="tpu_custom_call" | custom-call | bytes 16777216 | tf_op jit(solution)/shard_map/input_back/pallas_call | solution.py:504
  423.8 2.5 add_convert_fusion.4
  428.5 4.2 add_convert_fusion.1
  432.7 16.4 %collective-permute-done.25 = f32[1,3584]{1,0:T(1,128)S(1)} collective-permute-done((f32[1,3584]{1,0:T(1,128)S(1)}, f32[1,3584]{1,0:T(1,128)S(1)}, u32[]{:S(2)}, u32[]{:S(2)}) %collective-permute-start.25) | collective-permute-done | bytes 14368 | tf_op jit(solution)/shard_map/ppermute | solution.py:284
  449.8 16.4 %collective-permute-start.28 = (bf16[3,64,1280]{2,1,0:T(8,128)(2,1)S(1)}, bf16[3,64,1280]{2,1,0:T(8,128)(2,1)}, u32[]{:S(2)}, u32[]{:S(2)}) collective-permute-start(bf16[3,64,1280]{2,1,0:T(8,128)(2,1)S(1)} %dynamic-slice_bitcast_fusion.4), channel_id=1, source_target_pairs={{0,8},{2,10},{4,12},{6,14},{8,0},{10,2},{12,4},{14,6},{16,24},{18,... | collective-permute-start | bytes 1474568 | tf_op jit(solution)/shard_map/ppermute | solution.py:284
  466.1 15.6 %reduce-scatter.2.cloned.1.call-done = bf16[1,3,64,1024]{3,2,1,0:T(8,128)(2,1)} async-done(((bf16[16,3,64,1024]{3,2,1,0:T(8,128)(2,1)}), bf16[1,3,64,1024]{3,2,1,0:T(8,128)(2,1)}) %reduce-scatter.2.cloned.1.call-update) | async-done | bytes 393232 | tf_op jit(solution)/shard_map/reduce_scatter | solution.py:939
  481.9 4.7 collective-permute-start.27
  486.8 10.5 %collective-permute-done.29 = f32[1,3584]{1,0:T(1,128)S(1)} collective-permute-done((f32[1,3584]{1,0:T(1,128)S(1)}, f32[1,3584]{1,0:T(1,128)S(1)}, u32[]{:S(2)}, u32[]{:S(2)}) %collective-permute-start.29) | collective-permute-done | bytes 14368 | tf_op jit(solution)/shard_map/ppermute | solution.py:284
  499.7 3.5 collective-permute-start.31
  507.0 10.1 %collective-permute-start.33 = (bf16[4,64,512]{2,1,0:T(8,128)(2,1)S(1)}, bf16[4,64,512]{2,1,0:T(8,128)(2,1)S(1)}, u32[]{:S(2)}, u32[]{:S(2)}) collective-permute-start(bf16[4,64,512]{2,1,0:T(8,128)(2,1)S(1)} %dynamic-slice_bitcast_fusion.5), channel_id=1, source_target_pairs={{0,8},{2,10},{4,12},{6,14},{8,0},{10,2},{12,4},{14,6},{16,24},{18,... | collective-permute-start | bytes 786440 | tf_op jit(solution)/shard_map/ppermute | solution.py:284
  518.9 2.6 collective-permute-done.33
  (142 shorter events, 62.9 us)
Async XLA Ops:
  7.2 187.1 %all-gather.5.cloned.1.call-start = ((), (), s32[]{:S(2)}) async-start(), calls=%async_computation.2 | async-start | bytes 8355840 | tf_op jit(solution)/shard_map/all_gather | solution.py:907
  10.2 250.4 %all-gather.7.cloned.1.call-start = ((), (), s32[]{:S(2)}) async-start(), calls=%async_computation.3 | async-start | bytes 6684672 | tf_op jit(solution)/shard_map/all_gather | solution.py:908
  10.3 9.4 %collective-permute-start = (bf16[4,64,512]{2,1,0:T(8,128)(2,1)S(1)}, bf16[4,64,512]{2,1,0:T(8,128)(2,1)S(1)}, u32[]{:S(2)}, u32[]{:S(2)}) collective-permute-start(bf16[4,64,512]{2,1,0:T(8,128)(2,1)S(1)} %get-tuple-element.200), channel_id=1, source_target_pairs={{0,8},{2,10},{4,12},{6,14},{8,0},{10,2},{12,4},{14,6},{16,24},{18,... | collective-permute-start | bytes 786440 | tf_op jit(solution)/shard_map/ppermute | solution.py:284
  19.8 6.3 %collective-permute-start.1 = (bf16[2,4,64,512]{3,2,1,0:T(8,128)(2,1)S(1)}, bf16[2,4,64,512]{3,2,1,0:T(8,128)(2,1)}, u32[]{:S(2)}, u32[]{:S(2)}) collective-permute-start(bf16[2,4,64,512]{3,2,1,0:T(8,128)(2,1)S(1)} %maximum_select_fusion.3), channel_id=1, source_target_pairs={{8,16},{10,18},{12,20},{14,22},{16,8},{18,10},{20,12},{22,14},{9,1... | collective-permute-start | bytes 1572872 | tf_op jit(solution)/shard_map/ppermute | solution.py:293
  25.6 83.7 %collective-permute-start.5 = (bf16[1024,1024]{1,0:T(8,128)(2,1)}, bf16[1024,1024]{1,0:T(8,128)(2,1)}, u32[]{:S(2)}, u32[]{:S(2)}) collective-permute-start(bf16[1024,1024]{1,0:T(8,128)(2,1)} %norm.1.own), channel_id=1, source_target_pairs={{0,1},{1,0},{2,3},{3,2},{4,5},{5,4},{6,7},{7,6},{8,9},{9,8},{10,11... | collective-permute-start | bytes 6291464 | tf_op jit(solution)/shard_map/ppermute | solution.py:280
  25.6 83.7 %collective-permute-start.6 = (bf16[1024,1024]{1,0:T(8,128)(2,1)S(1)}, bf16[1024,1024]{1,0:T(8,128)(2,1)}, u32[]{:S(2)}, u32[]{:S(2)}) collective-permute-start(bf16[1024,1024]{1,0:T(8,128)(2,1)S(1)} %copy-done.1), channel_id=1, source_target_pairs={{0,1},{1,0},{2,3},{3,2},{4,5},{5,4},{6,7},{7,6},{8,9},{9,8},{10,11... | collective-permute-start | bytes 6291464 | tf_op jit(solution)/shard_map/ppermute | solution.py:280
  26.1 54.0 %collective-permute-start.2 = (bf16[2,4,64,512]{3,2,1,0:T(8,128)(2,1)}, bf16[2,4,64,512]{3,2,1,0:T(8,128)(2,1)}, u32[]{:S(2)}, u32[]{:S(2)}) collective-permute-start(bf16[2,4,64,512]{3,2,1,0:T(8,128)(2,1)} %collective-permute-done.1), channel_id=1, source_target_pairs={{8,0},{10,2},{12,4},{14,6},{16,24},{18,26},{20,28},{22,30},{9,1},{... | collective-permute-start | bytes 1572872 | tf_op jit(solution)/shard_map/ppermute | solution.py:293
  28.2 453.5 %reduce-scatter.2.cloned.1.call-start = ((), (), s32[]{:S(2)}) async-start(), calls=%async_computation.1 | async-start | bytes 6684672 | tf_op jit(solution)/shard_map/reduce_scatter | solution.py:939
  82.6 21.9 %collective-permute-start.4 = (bf16[4,2,64,512]{3,2,1,0:T(8,128)(2,1)}, bf16[4,2,64,512]{3,2,1,0:T(8,128)(2,1)}, u32[]{:S(2)}, u32[]{:S(2)}) collective-permute-start(bf16[4,2,64,512]{3,2,1,0:T(8,128)(2,1)} %get-tuple-element.197), channel_id=1, source_target_pairs={{0,2},{2,0},{4,6},{6,4},{8,10},{10,8},{12,14},{14,12},{16,18},{18,... | collective-permute-start | bytes 1572872 | tf_op jit(solution)/shard_map/ppermute | solution.py:284
  83.9 23.0 %collective-permute-start.3 = (bf16[4,2,64,512]{3,2,1,0:T(8,128)(2,1)}, bf16[4,2,64,512]{3,2,1,0:T(8,128)(2,1)}, u32[]{:S(2)}, u32[]{:S(2)}) collective-permute-start(bf16[4,2,64,512]{3,2,1,0:T(8,128)(2,1)} %get-tuple-element.198), channel_id=1, source_target_pairs={{0,4},{2,6},{4,0},{6,2},{8,12},{10,14},{12,8},{14,10},{16,20},{18,... | collective-permute-start | bytes 1572872 | tf_op jit(solution)/shard_map/ppermute | solution.py:284
  109.3 35.0 %collective-permute-start.7 = (bf16[2,4,2,64,512]{4,3,2,1,0:T(8,128)(2,1)}, bf16[2,4,2,64,512]{4,3,2,1,0:T(8,128)(2,1)S(1)}, u32[]{:S(2)}, u32[]{:S(2)}) collective-permute-start(bf16[2,4,2,64,512]{4,3,2,1,0:T(8,128)(2,1)} %maximum_select_fusion.1.first_own), channel_id=1, source_target_pairs={{0,2},{2,0},{4,6},{6,4},{8,10},{10,8},{12,14},{14,12},{16,18},{18,... | collective-permute-start | bytes 3145736 | tf_op jit(solution)/shard_map/ppermute | solution.py:284
  111.6 33.2 %collective-permute-start.8 = (bf16[2,4,2,64,512]{4,3,2,1,0:T(8,128)(2,1)}, bf16[2,4,2,64,512]{4,3,2,1,0:T(8,128)(2,1)S(1)}, u32[]{:S(2)}, u32[]{:S(2)}) collective-permute-start(bf16[2,4,2,64,512]{4,3,2,1,0:T(8,128)(2,1)} %maximum_select_fusion.2.second_own), channel_id=1, source_target_pairs={{0,4},{2,6},{4,0},{6,2},{8,12},{10,14},{12,8},{14,10},{16,20},{18,... | collective-permute-start | bytes 3145736 | tf_op jit(solution)/shard_map/ppermute | solution.py:284
  258.5 56.0 %collective-permute-start.12 = (bf16[2,4,3,64,768]{4,3,2,1,0:T(8,128)(2,1)}, bf16[2,4,3,64,768]{4,3,2,1,0:T(8,128)(2,1)S(1)}, u32[]{:S(2)}, u32[]{:S(2)}) collective-permute-start(bf16[2,4,3,64,768]{4,3,2,1,0:T(8,128)(2,1)} %get-tuple-element.111), channel_id=1, source_target_pairs={{0,4},{2,6},{4,0},{6,2},{8,12},{10,14},{12,8},{14,10},{16,20},{18,... | collective-permute-start | bytes 7077896 | tf_op jit(solution)/shard_map/ppermute | solution.py:284
  260.3 54.1 %collective-permute-start.11 = (bf16[2,4,3,64,512]{4,3,2,1,0:T(8,128)(2,1)}, bf16[2,4,3,64,512]{4,3,2,1,0:T(8,128)(2,1)}, u32[]{:S(2)}, u32[]{:S(2)}) collective-permute-start(bf16[2,4,3,64,512]{4,3,2,1,0:T(8,128)(2,1)} %get-tuple-element.110), channel_id=1, source_target_pairs={{0,2},{2,0},{4,6},{6,4},{8,10},{10,8},{12,14},{14,12},{16,18},{18,... | collective-permute-start | bytes 4718600 | tf_op jit(solution)/shard_map/ppermute | solution.py:284
  329.2 9.4 %collective-permute-start.16 = (bf16[1024,1024]{1,0:T(8,128)(2,1)}, bf16[1024,1024]{1,0:T(8,128)(2,1)}, u32[]{:S(2)}, u32[]{:S(2)}) collective-permute-start(bf16[1024,1024]{1,0:T(8,128)(2,1)} %get-tuple-element.125.own), channel_id=1, source_target_pairs={{0,1},{1,0},{2,3},{3,2},{4,5},{5,4},{6,7},{7,6},{8,9},{9,8},{10,11... | collective-permute-start | bytes 6291464 | tf_op jit(solution)/shard_map/ppermute | solution.py:280
  333.8 48.1 %collective-permute-start.14 = (bf16[4,3,64,768]{3,2,1,0:T(8,128)(2,1)}, bf16[4,3,64,768]{3,2,1,0:T(8,128)(2,1)}, u32[]{:S(2)}, u32[]{:S(2)}) collective-permute-start(bf16[4,3,64,768]{3,2,1,0:T(8,128)(2,1)} %dynamic-slice_bitcast_fusion), channel_id=1, source_target_pairs={{0,2},{2,0},{4,6},{6,4},{8,10},{10,8},{12,14},{14,12},{16,18},{18,... | collective-permute-start | bytes 3538952 | tf_op jit(solution)/shard_map/ppermute | solution.py:284
  338.5 43.4 %collective-permute-start.13 = (bf16[4,3,64,512]{3,2,1,0:T(8,128)(2,1)}, bf16[4,3,64,512]{3,2,1,0:T(8,128)(2,1)}, u32[]{:S(2)}, u32[]{:S(2)}) collective-permute-start(bf16[4,3,64,512]{3,2,1,0:T(8,128)(2,1)} %dynamic-slice_bitcast_fusion.1), channel_id=1, source_target_pairs={{0,4},{2,6},{4,0},{6,2},{8,12},{10,14},{12,8},{14,10},{16,20},{18,... | collective-permute-start | bytes 2359304 | tf_op jit(solution)/shard_map/ppermute | solution.py:284
  381.9 27.7 %collective-permute-start.20 = (bf16[1024,1024]{1,0:T(8,128)(2,1)}, bf16[1024,1024]{1,0:T(8,128)(2,1)}, u32[]{:S(2)}, u32[]{:S(2)}) collective-permute-start(bf16[1024,1024]{1,0:T(8,128)(2,1)} %get-tuple-element.144), channel_id=1, source_target_pairs={{0,1},{1,0},{2,3},{3,2},{4,5},{5,4},{6,7},{7,6},{8,9},{9,8},{10,11... | collective-permute-start | bytes 6291464 | tf_op jit(solution)/shard_map/ppermute | solution.py:280
  385.1 23.3 %collective-permute-start.19 = (bf16[2,3,64,1280]{3,2,1,0:T(8,128)(2,1)S(1)}, bf16[2,3,64,1280]{3,2,1,0:T(8,128)(2,1)S(1)}, u32[]{:S(2)}, u32[]{:S(2)}) collective-permute-start(bf16[2,3,64,1280]{3,2,1,0:T(8,128)(2,1)S(1)} %get-tuple-element.191), channel_id=1, source_target_pairs={{0,8},{2,10},{4,12},{6,14},{24,16},{26,18},{28,20},{30,22},{1,9},{... | collective-permute-start | bytes 2949128 | tf_op jit(solution)/shard_map/ppermute | solution.py:293
  386.6 41.9 %collective-permute-start.26 = (bf16[1024,1024]{1,0:T(8,128)(2,1)}, bf16[1024,1024]{1,0:T(8,128)(2,1)}, u32[]{:S(2)}, u32[]{:S(2)}) collective-permute-start(bf16[1024,1024]{1,0:T(8,128)(2,1)} %get-tuple-element.156), channel_id=1, source_target_pairs={{0,1},{1,0},{2,3},{3,2},{4,5},{5,4},{6,7},{7,6},{8,9},{9,8},{10,11... | collective-permute-start | bytes 6291464 | tf_op jit(solution)/shard_map/ppermute | solution.py:280
  387.1 31.8 %collective-permute-start.17 = (bf16[2,4,2,64,512]{4,3,2,1,0:T(8,128)(2,1)}, bf16[2,4,2,64,512]{4,3,2,1,0:T(8,128)(2,1)}, u32[]{:S(2)}, u32[]{:S(2)}) collective-permute-start(bf16[2,4,2,64,512]{4,3,2,1,0:T(8,128)(2,1)} %get-tuple-element.139), channel_id=1, source_target_pairs={{0,2},{2,0},{4,6},{6,4},{8,10},{10,8},{12,14},{14,12},{16,18},{18,... | collective-permute-start | bytes 3145736 | tf_op jit(solution)/shard_map/ppermute | solution.py:284
  388.1 31.1 %collective-permute-start.18 = (bf16[2,4,2,64,512]{4,3,2,1,0:T(8,128)(2,1)}, bf16[2,4,2,64,512]{4,3,2,1,0:T(8,128)(2,1)}, u32[]{:S(2)}, u32[]{:S(2)}) collective-permute-start(bf16[2,4,2,64,512]{4,3,2,1,0:T(8,128)(2,1)} %get-tuple-element.140), channel_id=1, source_target_pairs={{0,4},{2,6},{4,0},{6,2},{8,12},{10,14},{12,8},{14,10},{16,20},{18,... | collective-permute-start | bytes 3145736 | tf_op jit(solution)/shard_map/ppermute | solution.py:284
  419.2 8.3 %collective-permute-start.24 = (f32[1,3584]{1,0:T(1,128)S(1)}, f32[1,3584]{1,0:T(1,128)S(1)}, u32[]{:S(2)}, u32[]{:S(2)}) collective-permute-start(f32[1,3584]{1,0:T(1,128)S(1)} %pad_maximum_fusion.3), channel_id=1, source_target_pairs={{0,2},{2,0},{4,6},{6,4},{8,10},{10,8},{12,14},{14,12},{16,18},{18,... | collective-permute-start | bytes 43016 | tf_op jit(solution)/shard_map/ppermute | solution.py:284
  420.3 29.1 %collective-permute-start.23 = (bf16[2,3,64,1280]{3,2,1,0:T(8,128)(2,1)}, bf16[2,3,64,1280]{3,2,1,0:T(8,128)(2,1)S(1)}, u32[]{:S(2)}, u32[]{:S(2)}) collective-permute-start(bf16[2,3,64,1280]{3,2,1,0:T(8,128)(2,1)} %add_convert_fusion.6), channel_id=1, source_target_pairs={{8,16},{10,18},{12,20},{14,22},{16,8},{18,10},{20,12},{22,14},{9,1... | collective-permute-start | bytes 2949128 | tf_op jit(solution)/shard_map/ppermute | solution.py:293
  422.9 26.3 %collective-permute-start.22 = (bf16[4,2,64,512]{3,2,1,0:T(8,128)(2,1)S(1)}, bf16[4,2,64,512]{3,2,1,0:T(8,128)(2,1)S(1)}, u32[]{:S(2)}, u32[]{:S(2)}) collective-permute-start(bf16[4,2,64,512]{3,2,1,0:T(8,128)(2,1)S(1)} %dynamic-slice_bitcast_fusion.2), channel_id=1, source_target_pairs={{0,2},{2,0},{4,6},{6,4},{8,10},{10,8},{12,14},{14,12},{16,18},{18,... | collective-permute-start | bytes 1572872 | tf_op jit(solution)/shard_map/ppermute | solution.py:284
  426.3 23.0 %collective-permute-start.21 = (bf16[4,2,64,512]{3,2,1,0:T(8,128)(2,1)S(1)}, bf16[4,2,64,512]{3,2,1,0:T(8,128)(2,1)S(1)}, u32[]{:S(2)}, u32[]{:S(2)}) collective-permute-start(bf16[4,2,64,512]{3,2,1,0:T(8,128)(2,1)S(1)} %dynamic-slice_bitcast_fusion.3), channel_id=1, source_target_pairs={{0,4},{2,6},{4,0},{6,2},{8,12},{10,14},{12,8},{14,10},{16,20},{18,... | collective-permute-start | bytes 1572872 | tf_op jit(solution)/shard_map/ppermute | solution.py:284
  427.6 21.6 %collective-permute-start.25 = (f32[1,3584]{1,0:T(1,128)S(1)}, f32[1,3584]{1,0:T(1,128)S(1)}, u32[]{:S(2)}, u32[]{:S(2)}) collective-permute-start(f32[1,3584]{1,0:T(1,128)S(1)} %add.146), channel_id=1, source_target_pairs={{0,4},{2,6},{4,0},{6,2},{8,12},{10,14},{12,8},{14,10},{16,20},{18,... | collective-permute-start | bytes 43016 | tf_op jit(solution)/shard_map/ppermute | solution.py:284
  449.8 47.5 %collective-permute-start.28 = (bf16[3,64,1280]{2,1,0:T(8,128)(2,1)S(1)}, bf16[3,64,1280]{2,1,0:T(8,128)(2,1)}, u32[]{:S(2)}, u32[]{:S(2)}) collective-permute-start(bf16[3,64,1280]{2,1,0:T(8,128)(2,1)S(1)} %dynamic-slice_bitcast_fusion.4), channel_id=1, source_target_pairs={{0,8},{2,10},{4,12},{6,14},{8,0},{10,2},{12,4},{14,6},{16,24},{18,... | collective-permute-start | bytes 1474568 | tf_op jit(solution)/shard_map/ppermute | solution.py:284
  481.9 17.6 %collective-permute-start.27 = (bf16[2,4,64,512]{3,2,1,0:T(8,128)(2,1)S(1)}, bf16[2,4,64,512]{3,2,1,0:T(8,128)(2,1)S(1)}, u32[]{:S(2)}, u32[]{:S(2)}) collective-permute-start(bf16[2,4,64,512]{3,2,1,0:T(8,128)(2,1)S(1)} %get-tuple-element.193), channel_id=1, source_target_pairs={{0,8},{2,10},{4,12},{6,14},{24,16},{26,18},{28,20},{30,22},{1,9},{... | collective-permute-start | bytes 1572872 | tf_op jit(solution)/shard_map/ppermute | solution.py:293
  486.7 10.6 %collective-permute-start.29 = (f32[1,3584]{1,0:T(1,128)S(1)}, f32[1,3584]{1,0:T(1,128)S(1)}, u32[]{:S(2)}, u32[]{:S(2)}) collective-permute-start(f32[1,3584]{1,0:T(1,128)S(1)} %add.147), channel_id=1, source_target_pairs={{0,8},{2,10},{4,12},{6,14},{8,0},{10,2},{12,4},{14,6},{16,24},{18,... | collective-permute-start | bytes 43016 | tf_op jit(solution)/shard_map/ppermute | solution.py:284
  499.7 7.1 %collective-permute-start.31 = (f32[1,3584]{1,0:T(1,128)S(1)}, f32[1,3584]{1,0:T(1,128)S(1)}, u32[]{:S(2)}, u32[]{:S(2)}) collective-permute-start(f32[1,3584]{1,0:T(1,128)S(1)} %add.154), channel_id=1, source_target_pairs={{0,16},{2,18},{4,20},{6,22},{8,24},{10,26},{12,28},{14,30},{16,0},... | collective-permute-start | bytes 43016 | tf_op jit(solution)/shard_map/ppermute | solution.py:284
  507.0 14.5 %collective-permute-start.33 = (bf16[4,64,512]{2,1,0:T(8,128)(2,1)S(1)}, bf16[4,64,512]{2,1,0:T(8,128)(2,1)S(1)}, u32[]{:S(2)}, u32[]{:S(2)}) collective-permute-start(bf16[4,64,512]{2,1,0:T(8,128)(2,1)S(1)} %dynamic-slice_bitcast_fusion.5), channel_id=1, source_target_pairs={{0,8},{2,10},{4,12},{6,14},{8,0},{10,2},{12,4},{14,6},{16,24},{18,... | collective-permute-start | bytes 786440 | tf_op jit(solution)/shard_map/ppermute | solution.py:284
  (21 other events, 95.6 us)
Sparse Core Ops, SparseCore 0:
  10.8 145.7 all-gather.4
  160.0 93.2 all-gather.6
  314.6 167.0 reduce-scatter.1
